TPU v7x, 32 devices: a whole 2x2x4 slice. The times are simulated.
32 devices in a mesh: seq: 8 (over z, x), head: 4 (over y, core).
Axes of the slice: x: 2, y: 2, z: 4, core: 2. Of those that a mesh axis runs over, the one named last changes fastest.
Arguments:
- q_in: bfloat16 [16384, 2048], P(('seq', 'head')), may hold values from -6 to 6
- k_in: bfloat16 [16384, 2048], P(('seq', 'head')), may hold values from -6 to 6
- v_in: bfloat16 [16384, 2048], P(('seq', 'head')), may hold values from -6 to 6
- beta: bfloat16 [16384, 16], P(('seq', 'head')), may hold values from 0 to 1, as said below
- conv_q: float32 [4, 2048], replicated, may hold values from -3 to 3
- conv_k: float32 [4, 2048], replicated, may hold values from -3 to 3
- conv_v: float32 [4, 2048], replicated, may hold values from -3 to 3
- out_gain: float32 [128], replicated, may hold values from 0.25 to 1.75
Outputs:
- mixed: bfloat16 [16384, 2048], P(('seq', 'head'))
Inputs may be any that keep to these rules, and one draw needn't show every extreme that they name: `beta`: write strengths of the delta rule, positive.
All inputs are finite; a program needn't handle non-finite values.
Results may differ from a plain program's by a relative error of at most 0.001.
Values may be sent and summed in bfloat16 or wider, within the bound.
A program may use at most 576 MiB of HBM per device.

v0:
```python
import jax
import jax.numpy as jnp
from jax import lax
from jax.sharding import PartitionSpec as P

KEY_WIDTH = 128
DV = 128
BLOCK = 64
KW = 4


peak_level = lax.Precision.HIGHEST


def shifted(value, axis, by):
    peers = lax.axis_size(axis)
    pairs = [(i, i + by) for i in range(peers) if 0 <= i + by < peers]
    return lax.ppermute(value, axis, pairs)


def causal_conv(padded, weight, length):
    summed = weight[0] * padded[0:length]
    for offset in range(1, weight.shape[0]):
        summed = summed + weight[offset] * padded[offset : offset + length]
    return summed


def unit_rows(vectors):
    return vectors / jnp.sqrt(jnp.sum(vectors * vectors, axis=-1, keepdims=True) + 1e-06)


def features(q_pad, k_pad, v_pad, beta_rows, conv_q, conv_k, conv_v):
    length = beta_rows.shape[0]
    head_count = beta_rows.shape[1]
    q_conv = causal_conv(q_pad.astype(jnp.float32), conv_q, length)
    k_conv = causal_conv(k_pad.astype(jnp.float32), conv_k, length)
    v_conv = causal_conv(v_pad.astype(jnp.float32), conv_v, length)
    queries = unit_rows(jax.nn.silu(q_conv).reshape(length, head_count, -1))
    key_rows = unit_rows(jax.nn.silu(k_conv).reshape(length, head_count, -1))
    values = jax.nn.silu(v_conv).reshape(length, head_count, -1)
    return (queries, key_rows, values, beta_rows.astype(jnp.float32))


def block_parts(queries, key_rows, values, surge_strength):
    length, head_count, ignored = key_rows.shape
    block_count = length // BLOCK

    def to_blocks(matrix):
        return jnp.swapaxes(matrix.reshape(block_count, BLOCK, head_count, matrix.shape[-1]), 1, 2)

    query_tiles = to_blocks(queries)
    key_tiles = to_blocks(key_rows)
    v_blocks = to_blocks(values)
    s_blocks = jnp.swapaxes(surge_strength.reshape(block_count, BLOCK, head_count), 1, 2)[..., None]
    scaled_k = key_tiles * s_blocks
    gram_rows = jnp.einsum("nhik,nhjk->nhij", scaled_k, key_tiles, precision=peak_level)
    system = jnp.tril(gram_rows, -1) + jnp.eye(BLOCK, dtype=gram_rows.dtype)
    weight_rows = lax.linalg.triangular_solve(
        system, scaled_k, left_side=True, lower=True, unit_diagonal=True
    )
    update_rows = lax.linalg.triangular_solve(
        system, v_blocks * s_blocks, left_side=True, lower=True, unit_diagonal=True
    )
    attention_scores = jnp.tril(
        jnp.einsum("nhik,nhjk->nhij", query_tiles, key_tiles, precision=peak_level)
    )
    return (query_tiles, key_tiles, weight_rows, update_rows, attention_scores)


def run_blocks(carried, parts):

    def run_advance(present_value, pieces):
        query_tiles, key_tiles, weight_rows, update_rows, attention_scores = pieces
        fresh_values = update_rows - jnp.einsum(
            "jel,jlm->jem", weight_rows, present_value, precision=peak_level
        )
        blended_rows = jnp.einsum(
            "jel,jlm->jem", query_tiles, present_value, precision=peak_level
        ) + jnp.einsum("ezq,eqd->ezd", attention_scores, fresh_values, precision=peak_level)
        present_value = present_value + jnp.einsum(
            "pty,ptn->pyn", key_tiles, fresh_values, precision=peak_level
        )
        return (present_value, blended_rows)

    ignored, outputs = lax.scan(run_advance, carried, parts)
    block_count, head_count, rows_block, width = outputs.shape
    return jnp.swapaxes(outputs, 1, 2).reshape(block_count * rows_block, head_count, width)


def finish(outputs, out_gain):
    inv_rms = lax.rsqrt(jnp.mean(outputs * outputs, axis=-1, keepdims=True) + 1e-05)
    return (outputs * inv_rms * out_gain).reshape(outputs.shape[0], -1).astype(jnp.bfloat16)


def identity_pair(head_count):
    eye_block = jnp.broadcast_to(
        jnp.eye(KEY_WIDTH, dtype=jnp.float32), (head_count, KEY_WIDTH, KEY_WIDTH)
    )
    return (eye_block, jnp.zeros((head_count, KEY_WIDTH, DV), jnp.float32))


def summarize(parts, head_count):

    def summarize_advance(carried, pieces):
        transfer, shifted_state = carried
        query_tiles, key_tiles, weight_rows, update_rows, attention_scores = pieces
        fresh_values = update_rows - jnp.einsum(
            "jel,jlm->jem", weight_rows, shifted_state, precision=peak_level
        )
        shifted_state = shifted_state + jnp.einsum(
            "pty,ptn->pyn", key_tiles, fresh_values, precision=peak_level
        )
        moved = jnp.einsum("hck,hkj->hcj", weight_rows, transfer, precision=peak_level)
        transfer = transfer - jnp.einsum("hck,hcj->hkj", key_tiles, moved, precision=peak_level)
        return ((transfer, shifted_state), None)

    summary, ignored = lax.scan(summarize_advance, identity_pair(head_count), parts)
    return summary


def local_parts(q_rows, k_rows, v_rows, beta_rows, rims, conv_q, conv_k, conv_v):
    q_pad = jnp.concatenate([rims[0], q_rows], axis=0)
    k_pad = jnp.concatenate([rims[1], k_rows], axis=0)
    v_pad = jnp.concatenate([rims[2], v_rows], axis=0)
    return block_parts(*features(q_pad, k_pad, v_pad, beta_rows, conv_q, conv_k, conv_v))


def shards(q_in, k_in, v_in, beta, conv_q, conv_k, conv_v, out_gain):
    edge = KW - 1
    q_rows, k_rows, v_rows, beta_rows = (
        lax.all_to_all(q_in, "head", split_axis=1, concat_axis=0, tiled=True),
        lax.all_to_all(k_in, "head", split_axis=1, concat_axis=0, tiled=True),
        lax.all_to_all(v_in, "head", split_axis=1, concat_axis=0, tiled=True),
        lax.all_to_all(beta, "head", split_axis=1, concat_axis=0, tiled=True),
    )
    local_heads = beta_rows.shape[1]
    start = lax.axis_index("head") * (local_heads * KEY_WIDTH)
    conv_qh = lax.dynamic_slice_in_dim(conv_q, start, local_heads * KEY_WIDTH, 1)
    conv_kh = lax.dynamic_slice_in_dim(conv_k, start, local_heads * KEY_WIDTH, 1)
    conv_vh = lax.dynamic_slice_in_dim(conv_v, start, local_heads * DV, 1)
    rim_stack = jnp.stack([q_rows[-edge:], k_rows[-edge:], v_rows[-edge:]])
    rims = shifted(rim_stack, "seq", 1)
    parts = local_parts(q_rows, k_rows, v_rows, beta_rows, rims, conv_qh, conv_kh, conv_vh)
    transfer, shifted_state = summarize(parts, local_heads)

    def forward(turn, incoming):
        outgoing = (
            jnp.einsum("hij,hjv->hiv", transfer, incoming, precision=peak_level) + shifted_state
        )
        return shifted(outgoing, "seq", 1)

    incoming = lax.fori_loop(0, lax.axis_size("seq") - 1, forward, jnp.zeros_like(shifted_state))
    normed = finish(run_blocks(incoming, parts), out_gain)
    return lax.all_to_all(normed, "head", split_axis=0, concat_axis=1, tiled=True)


def solution(mesh):
    in_specs = (
        P(("seq", "head"), None),
        P(("seq", "head"), None),
        P(("seq", "head"), None),
        P(("seq", "head"), None),
        P(),
        P(),
        P(),
        P(),
    )
    out_specs = P(("seq", "head"), None)
    return jax.shard_map(shards, mesh=mesh, in_specs=in_specs, out_specs=out_specs, check_vma=False)
```

profile of v0, /device:TPU:27, one launch (start us, length us, event | category | flops | bytes accessed | tf_op | source)
XLA Modules:
  0.0 1036.3 jit_solution(62303984522287462)
XLA Ops:
  12.1 20.9 %all-to-all-done.1 = bf16[512,4,512]{0,2,1:T(8,128)(2,1)S(1)} async-done(((bf16[512,4,512]{0,2,1:T(8,128)(2,1)}), bf16[512,4,512]{0,2,1:T(8,128)(2,1)S(1)}, u32[]{:S(2)}, u32[]{:S(2)}) %all-to-all-start.1) | async-done | bytes 2097184 | tf_op jit(solution)/shard_map/all_to_all | solution.py:132
  42.2 21.0 %all-to-all-done.2 = bf16[512,4,512]{0,2,1:T(8,128)(2,1)} async-done(((bf16[512,4,512]{0,2,1:T(8,128)(2,1)}), bf16[512,4,512]{0,2,1:T(8,128)(2,1)}, u32[]{:S(2)}, u32[]{:S(2)}) %all-to-all-start.2) | async-done | bytes 2097184 | tf_op jit(solution)/shard_map/all_to_all | solution.py:133
  79.4 14.1 %all-to-all-done = bf16[512,4,512]{0,2,1:T(8,128)(2,1)} async-done(((bf16[512,4,512]{0,2,1:T(8,128)(2,1)}), bf16[512,4,512]{0,2,1:T(8,128)(2,1)}, u32[]{:S(2)}, u32[]{:S(2)}) %all-to-all-start) | async-done | bytes 2097184 | tf_op jit(solution)/shard_map/all_to_all | solution.py:131
  171.3 8.4 fusion.56
  179.7 7.0 copy.144
  186.7 6.5 broadcast_select_fusion
  193.2 7.3 copy.146
  200.5 12.4 %fusion.34 = f32[32,4,64,64]{3,2,1,0:T(8,128)} fusion(f32[32,4,64,128]{3,2,1,0:T(8,128)} %copy-done.2, f32[32,4,64]{2,1,0:T(4,128)S(1)} %copy.135), kind=kOutput, calls=%fused_computation.42 | convolution fusion | flops 806354944 | bytes 6324224 | tf_op jit(solution)/shard_map/nhik,nhjk->nhij/dot_general | solution.py:56
  212.9 7.2 copy.136
  220.2 7.9 add_bitcast_fusion
  228.1 265.2 %custom-call.5 = f32[32,4,1,64,64]{0,3,4,2,1:T(8,128)} custom-call(f32[32,4,1,64,64]{0,4,3,2,1:T(8,128)} %add_bitcast_fusion), custom_call_target="InvertDiagBlocksLowerTriangular" | custom-call | tf_op jit(solution)/shard_map/triangular_solve/custom-call.1 | solution.py:58
  493.3 8.7 copy.138
  511.9 9.9 fusion.32
  528.0 182.0 %while.37 = (s32[]{:T(128)}, f32[4,128,128]{2,1,0:T(8,128)S(1)}, f32[4,128,128]{2,1,0:T(8,128)S(1)}, f32[32,4,64,128]{3,2,1,0:T(8,128)}, f32[32,4,64,128]{3,2,1,...) while((s32[]{:T(128)}, f32[4,128,128]{2,1,0:T(8,128)S(1)}, ...), condition=%wide.region_2.4_spmd.clone, body=%wide.region_1.0_spmd.clone.sunk | while | flops 201621504 | bytes 2755168 | solution.py:117
  710.0 60.8 %while.35 = (s32[]{:T(128)}, f32[4,128,128]{2,1,0:T(8,128)S(1)}, f32[4,128,128]{2,1,0:T(8,128)S(1)}, f32[4,128,128]{2,1,0:T(8,128)S(1)}, s32[]{:T(128)}) while((s32[]{:T(128)}, f32[4,128,128]{2,1,0:T(8,128)S(1)}, f32[4,128,128]{2,1,0:T(8,128)S(1)}, f32[4,128,128]{2,1,0:T(8,128)S(1)}, s32[]{:T(128)}) %tuple.81), condition=%wide.region_4.6_spmd, body=%wide.region_3.5_spmd.sunk | while | flops 100728832 | bytes 2097253 | solution.py:152
  711.7 7.2 collective-permute-done
  720.6 7.2 collective-permute-done
  737.6 6.7 collective-permute-done
  746.0 6.7 collective-permute-done
  754.5 6.7 collective-permute-done
  762.9 7.9 collective-permute-done
  770.8 190.8 %while.36 = (s32[]{:T(128)}, f32[4,128,128]{2,1,0:T(8,128)S(1)}, f32[32,4,64,128]{3,2,1,0:T(8,128)}, f32[32,4,64,128]{3,2,1,0:T(8,128)}, f32[32,4,64,128]{3,2,1,...) while((s32[]{:T(128)}, f32[4,128,128]{2,1,0:T(8,128)S(1)}, ...), condition=%wide.region_7.9_spmd, body=%wide.region_6.8_spmd.sunk | while | flops 176291840 | bytes 2493533 | solution.py:85
  974.7 7.8 copy.147
  992.6 37.0 %all_to_all.86 = bf16[4,512,512]{2,1,0:T(8,128)(2,1)S(1)} all-to-all(bf16[4,512,512]{2,1,0:T(8,128)(2,1)S(1)} %multiply_convert_fusion), channel_id=1, replica_groups=mesh['seq'=8,'head'=4] {'head'}, dimensions={0} | all-to-all | bytes 4194304 | tf_op jit(solution)/shard_map/all_to_all | solution.py:154
  (364 shorter events, 549.2 us)
Async XLA Ops:
  0.0 73.0 %copy-start = (f32[128]{0:T(128)S(1)}, f32[128]{0:T(128)}, u32[]{:S(2)}) copy-start(f32[128]{0:T(128)} %param.23) | copy-start | bytes 1540
  3.9 29.1 %all-to-all-start.1 = ((bf16[512,4,512]{0,2,1:T(8,128)(2,1)}), bf16[512,4,512]{0,2,1:T(8,128)(2,1)S(1)}, u32[]{:S(2)}, u32[]{:S(2)}) async-start(bf16[512,4,512]{0,2,1:T(8,128)(2,1)} %bitcast.158), calls=%async_computation.1 | async-start | bytes 4194304 | tf_op jit(solution)/shard_map/all_to_all | solution.py:132
  33.0 30.2 %all-to-all-start.2 = ((bf16[512,4,512]{0,2,1:T(8,128)(2,1)}), bf16[512,4,512]{0,2,1:T(8,128)(2,1)}, u32[]{:S(2)}, u32[]{:S(2)}) async-start(bf16[512,4,512]{0,2,1:T(8,128)(2,1)} %bitcast.157), calls=%async_computation.2 | async-start | bytes 4194304 | tf_op jit(solution)/shard_map/all_to_all | solution.py:133
  38.3 30.2 %copy-start.10 = (bf16[512,16]{0,1:T(8,128)(2,1)S(1)}, bf16[512,16]{0,1:T(8,128)(2,1)}, u32[]{:S(2)}) copy-start(bf16[512,16]{0,1:T(8,128)(2,1)} %param.19) | copy-start | bytes 49156
  63.2 30.2 %all-to-all-start = ((bf16[512,4,512]{0,2,1:T(8,128)(2,1)}), bf16[512,4,512]{0,2,1:T(8,128)(2,1)}, u32[]{:S(2)}, u32[]{:S(2)}) async-start(bf16[512,4,512]{0,2,1:T(8,128)(2,1)} %bitcast.156), calls=%async_computation | async-start | bytes 4194304 | tf_op jit(solution)/shard_map/all_to_all | solution.py:131
  93.5 11.4 %all-to-all-start.3 = ((bf16[512,4,4]{0,2,1:T(4,128)(2,1)}), bf16[512,4,4]{0,2,1:T(4,128)(2,1)S(1)}, u32[]{:S(2)}, u32[]{:S(2)}) async-start(bf16[512,4,4]{0,2,1:T(4,128)(2,1)} %all_to_all.76), calls=%async_computation.3 | async-start | bytes 32768 | tf_op jit(solution)/shard_map/all_to_all | solution.py:134
  103.1 4.4 collective-permute-start.1
  164.5 3.7 copy-start.5
  169.3 2.0 copy-start.2
  212.9 7.3 copy-start.7
  212.9 7.3 copy-start.8
  212.9 7.3 copy-start.9
  511.9 9.9 copy-start.3
  511.9 9.9 copy-start.4
  521.8 6.2 copy-start.6
  710.4 8.5 collective-permute-start
  719.3 8.5 collective-permute-start
  728.2 7.7 collective-permute-start
  736.3 8.0 collective-permute-start
  744.7 8.0 collective-permute-start
  753.2 8.0 collective-permute-start
  761.6 9.2 collective-permute-start
  982.5 5.6 copy-start.14
  1029.6 6.3 copy-start.1
  (3 other events, 2.0 us)
where the time goes:
time: 1050 us; the launch traced here: 1040 us
  matrix products  410 us (39%)
  other arithmetic  329 us (31%)
  local copies, waits for them, and re-layouts  120 us (11%)
  waiting for transfers between devices  107 us (10%)
  blocking collectives  37 us (4%)
  starting transfers between devices  29.7 us (3%)
    another operation x5, other arithmetic, block_parts(): lax.linalg.triangular_solve(system, scaled_k, left_side=True, lower=True,...  274 us
    dot_general x32, matrix products, run_advance(): jnp.einsum('jel,jlm->jem', query_tiles, present_value, precision=peak_level)  61.6 us
    ppermute x8, waiting for transfers between devices, shifted(): return lax.ppermute(value, axis, pairs)  51.3 us
    dot_general x32, matrix products, summarize_advance(): jnp.einsum('pty,ptn->pyn', key_tiles, fresh_values, precision=peak_level)  48.9 us
    dot_general x32, matrix products, summarize_advance(): jnp.einsum('hck,hcj->hkj', key_tiles, moved, precision=peak_level)  48.6 us
    dot_general x32, matrix products, run_advance(): jnp.einsum('pty,ptn->pyn', key_tiles, fresh_values, precision=peak_level)  48.3 us
    dot_general x32, matrix products, run_advance(): jnp.einsum('jel,jlm->jem', weight_rows, present_value, precision=peak_level)  42.5 us
    dot_general x32, matrix products, summarize_advance(): jnp.einsum('jel,jlm->jem', weight_rows, shifted_state, precision=peak_level)  42.5 us
  transfers between devices with their start and end apart: 12, of which 11 were waited for; matrix products, arithmetic and copies ran while one was open for 2% of the time, Pallas kernels for 0%

commit v1 on v0

v1 whole, which is shorter than its diff:
```python
import functools
import jax
import jax.numpy as jnp
from jax import lax
from jax.experimental import pallas as pl
from jax.experimental.pallas import tpu as pltpu
from jax.sharding import PartitionSpec as P

WIDTH = 128
CHUNK = 128
KW = 4
RIM = 16
BASE = 8
HEADS_PER_STEP = 2

F32 = jnp.float32
BF16 = jnp.bfloat16
peak_level = lax.Precision.HIGHEST


def split(x):
    hi = x.astype(BF16)
    return hi, (x - hi.astype(F32)).astype(BF16)


def dot(a, b):
    return jnp.dot(a, b, preferred_element_type=F32)


def wide_left(a):
    hi, lo = split(a)
    return jnp.concatenate([hi, lo], axis=1)


def square_right(b):
    row = jnp.concatenate(split(b), axis=1)
    return jnp.concatenate([row, row], axis=0)


def fold(x):
    return x[:, :WIDTH] + x[:, WIDTH:]


def mm_square(a, b):
    return fold(dot(wide_left(a), square_right(b)))


def mm_wide(a, b):
    hi, lo = split(b)
    left = wide_left(a)
    return dot(left, jnp.concatenate([hi, hi], axis=0)) + dot(left[:, : a.shape[1]], lo)


def gram(rows, keys):
    hi, lo = split(keys)
    right = jnp.concatenate(
        [jnp.concatenate([hi, hi], axis=1), jnp.concatenate([lo, lo], axis=1)], axis=0
    )
    out = lax.dot_general(
        wide_left(rows), right, (((1,), (1,)), ((), ())), preferred_element_type=F32
    )
    return fold(out)


def lower_inverse(g):
    lane = lax.broadcasted_iota(jnp.int32, (BASE, CHUNK), 1)
    sub = lax.broadcasted_iota(jnp.int32, (BASE, CHUNK), 0)
    groups = CHUNK // BASE
    packed = jnp.zeros((BASE, CHUNK), F32)
    for i in range(groups):
        packed = jnp.where(lane // BASE == i, g[i * BASE : (i + 1) * BASE, :], packed)
    x = jnp.where(lane % BASE == sub, 1.0, 0.0).astype(F32)
    for j in range(BASE - 1):
        column = jnp.where(lane % BASE == j, packed, 0.0)
        if j:
            column = pltpu.roll(column, CHUNK - j, 1)
        for by in (1, 2, 4):
            column = column + pltpu.roll(column, by, 1)
        x = x - column * jnp.broadcast_to(x[j : j + 1, :], (BASE, CHUNK))
    inv = jnp.concatenate(
        [jnp.where(lane // BASE == i, x, 0.0) for i in range(groups)], axis=0
    )
    col = lax.broadcasted_iota(jnp.int32, (CHUNK, CHUNK), 1)
    row = lax.broadcasted_iota(jnp.int32, (CHUNK, CHUNK), 0)
    size = BASE
    while size < CHUNK:
        pairs = CHUNK // (2 * size)
        low = [slice((2 * p + 1) * size, (2 * p + 2) * size) for p in range(pairs)]
        up = [slice(2 * p * size, (2 * p + 1) * size) for p in range(pairs)]
        corner = jnp.where(col // size == row // size - 1, g, 0.0)
        corner = jnp.concatenate([corner[s] for s in low], axis=0)
        old = jnp.concatenate([inv[s] for s in low], axis=0)
        e = mm_square(corner, inv)
        zero = jnp.zeros((size, CHUNK), F32)
        e_full = jnp.concatenate(
            [t for p in range(pairs) for t in (zero, e[p * size : (p + 1) * size])], axis=0
        )
        new = old - mm_square(old, e_full)
        inv = jnp.concatenate(
            [t for p in range(pairs) for t in (inv[up[p]], new[p * size : (p + 1) * size])],
            axis=0,
        )
        size *= 2
    return inv


def conv_silu(x_ref, rim_ref, w_ref, pad, lanes):
    length = x_ref.shape[0]
    pad[0:RIM, :] = rim_ref[:, lanes].astype(F32)
    pad[RIM : RIM + length, :] = x_ref[:, lanes].astype(F32)
    w = w_ref[:, lanes]
    first = RIM - (KW - 1)
    summed = w[0:1, :] * pad[first : first + length, :]
    for j in range(1, KW):
        summed = summed + w[j : j + 1, :] * pad[first + j : first + j + length, :]
    return summed / (1.0 + jnp.exp(-summed))


def unit_rows(x):
    return x * lax.rsqrt(jnp.sum(x * x, axis=-1, keepdims=True) + 1e-06)


def local_kernel(q_ref, k_ref, v_ref, b_ref, qr_ref, kr_ref, vr_ref, cq_ref, ck_ref, cv_ref,
                 out_ref, sum_ref, *pads):
    length = q_ref.shape[0]
    step = pl.program_id(0)
    chunks = length // CHUNK
    row = lax.broadcasted_iota(jnp.int32, (CHUNK, CHUNK), 0)
    col = lax.broadcasted_iota(jnp.int32, (CHUNK, CHUNK), 1)
    beta = b_ref[...]
    which = lax.broadcasted_iota(jnp.int32, beta.shape, 1)
    prepared = []
    for i in range(HEADS_PER_STEP):
        lanes = slice(i * WIDTH, (i + 1) * WIDTH)
        q = unit_rows(conv_silu(q_ref, qr_ref, cq_ref, pads[3 * i], lanes))
        k = unit_rows(conv_silu(k_ref, kr_ref, ck_ref, pads[3 * i + 1], lanes))
        v = conv_silu(v_ref, vr_ref, cv_ref, pads[3 * i + 2], lanes)
        head = step * HEADS_PER_STEP + i
        b = jnp.sum(jnp.where(which == head, beta, 0.0), axis=1, keepdims=True)
        parts = []
        for n in range(chunks):
            rows = slice(n * CHUNK, (n + 1) * CHUNK)
            qn, kn, vn, bn = q[rows], k[rows], v[rows], b[rows]
            both = gram(jnp.concatenate([qn, kn], axis=0), kn)
            p = jnp.where(row >= col, both[:CHUNK], 0.0)
            g = jnp.where(row > col, both[CHUNK:] * bn, 0.0)
            inv = lower_inverse(g)
            wu = mm_wide(inv, jnp.concatenate([kn * bn, vn * bn], axis=1))
            parts.append((qn, jnp.concatenate([p, kn.T], axis=0), wu))
        prepared.append(parts)
    zero = jnp.zeros((CHUNK, WIDTH), F32)
    carried = [None] * HEADS_PER_STEP
    for n in range(chunks):
        for i in range(HEADS_PER_STEP):
            qn, pk, wu = prepared[i][n]
            w, u = wu[:, :WIDTH], wu[:, WIDTH:]
            if n == 0:
                fresh = jnp.concatenate([-w, u], axis=1)
                seen = jnp.concatenate([qn, zero], axis=1)
                eye = jnp.where(row == col, 1.0, 0.0).astype(F32)
                state = jnp.concatenate([eye, zero], axis=1)
            else:
                state = carried[i]
                moved = mm_wide(jnp.concatenate([w, qn], axis=0), state)
                fresh = jnp.concatenate([zero, u], axis=1) - moved[:CHUNK]
                seen = moved[CHUNK:]
            added = mm_wide(pk, fresh)
            out_ref[i, n * CHUNK : (n + 1) * CHUNK, :] = seen + added[:CHUNK]
            carried[i] = state + added[CHUNK:]
    for i in range(HEADS_PER_STEP):
        sum_ref[i, :, :] = carried[i]


def local_pass(q, k, v, beta, rims, conv_q, conv_k, conv_v):
    length, total = q.shape
    heads = total // WIDTH
    wide = HEADS_PER_STEP * WIDTH
    rows = pl.BlockSpec((length, wide), lambda h: (0, h))
    rim = pl.BlockSpec((RIM, wide), lambda h: (0, h))
    taps = pl.BlockSpec((KW, wide), lambda h: (0, h))
    return pl.pallas_call(
        local_kernel,
        grid=(heads // HEADS_PER_STEP,),
        in_specs=[rows, rows, rows, pl.BlockSpec((length, heads), lambda h: (0, 0)),
                  rim, rim, rim, taps, taps, taps],
        out_specs=[
            pl.BlockSpec((HEADS_PER_STEP, length, 2 * WIDTH), lambda h: (h, 0, 0)),
            pl.BlockSpec((HEADS_PER_STEP, WIDTH, 2 * WIDTH), lambda h: (h, 0, 0)),
        ],
        out_shape=[
            jax.ShapeDtypeStruct((heads, length, 2 * WIDTH), F32),
            jax.ShapeDtypeStruct((heads, WIDTH, 2 * WIDTH), F32),
        ],
        scratch_shapes=[pltpu.VMEM((RIM + length, WIDTH), F32)] * (3 * HEADS_PER_STEP),
        compiler_params=pltpu.CompilerParams(vmem_limit_bytes=48 * 2**20),
        name="local_pass",
    )(q, k, v, beta, *rims, conv_q, conv_k, conv_v)


def finish_kernel(part_ref, state_ref, gain_ref, out_ref):
    for i in range(part_ref.shape[0]):
        part = part_ref[i]
        o = part[:, WIDTH:] + mm_square(part[:, :WIDTH], state_ref[i])
        scale = lax.rsqrt(jnp.mean(o * o, axis=-1, keepdims=True) + 1e-05)
        out_ref[:, i * WIDTH : (i + 1) * WIDTH] = (o * scale * gain_ref[...]).astype(BF16)


def finish_pass(parts, states, gain):
    heads, length, ignored = parts.shape
    per = 2
    return pl.pallas_call(
        finish_kernel,
        grid=(heads // per,),
        in_specs=[
            pl.BlockSpec((per, length, 2 * WIDTH), lambda h: (h, 0, 0)),
            pl.BlockSpec((per, WIDTH, WIDTH), lambda h: (h, 0, 0)),
            pl.BlockSpec((1, WIDTH), lambda h: (0, 0)),
        ],
        out_specs=pl.BlockSpec((length, per * WIDTH), lambda h: (0, h)),
        out_shape=jax.ShapeDtypeStruct((length, heads * WIDTH), BF16),
        compiler_params=pltpu.CompilerParams(vmem_limit_bytes=48 * 2**20),
        name="finish_pass",
    )(parts, states, gain.reshape(1, WIDTH))


def shifted(value, axis):
    peers = lax.axis_size(axis)
    return lax.ppermute(value, axis, [(i, i + 1) for i in range(peers - 1)])


def times(a, b):
    return jnp.einsum("hij,hjv->hiv", a, b, precision=peak_level)


def incoming_states(summary):
    group = lax.axis_size("head")
    held = lax.all_to_all(summary, "head", split_axis=0, concat_axis=0, tiled=True)
    held = held.reshape(group, -1, WIDTH, 2 * WIDTH)
    before = [None, held[0]]
    for c in range(1, group):
        moved = times(held[c][:, :, :WIDTH], before[-1])
        before.append(moved.at[:, :, WIDTH:].add(held[c][:, :, WIDTH:]))
    transfer, local = before[-1][:, :, :WIDTH], before[-1][:, :, WIDTH:]
    arrived = jnp.zeros_like(local)
    for ignored in range(lax.axis_size("seq") - 1):
        arrived = shifted(times(transfer, arrived) + local, "seq")
    states = [arrived]
    for c in range(1, group):
        states.append(times(before[c][:, :, :WIDTH], arrived) + before[c][:, :, WIDTH:])
    states = jnp.concatenate(states, axis=0)
    return lax.all_to_all(states, "head", split_axis=0, concat_axis=0, tiled=True)


def shards(q_in, k_in, v_in, beta, conv_q, conv_k, conv_v, out_gain):
    edges = jnp.stack([q_in[-RIM:], k_in[-RIM:], v_in[-RIM:]])
    rims = shifted(edges, ("seq", "head"))
    parts, summary = local_pass(
        q_in, k_in, v_in, beta.astype(F32), [rims[0], rims[1], rims[2]], conv_q, conv_k, conv_v
    )
    return finish_pass(parts, incoming_states(summary), out_gain)


def solution(mesh):
    rows = P(("seq", "head"), None)
    in_specs = (rows, rows, rows, rows, P(), P(), P(), P())
    return jax.shard_map(
        shards, mesh=mesh, in_specs=in_specs, out_specs=rows, check_vma=False
    )
```

time: 1050 us -> 268 us (0.26)
  matrix products: 410 us -> 5.69 us
  other arithmetic: 329 us -> 0.23 us
  Pallas kernels: 0 us -> 134 us
  local copies, waits for them, and re-layouts: 120 us -> 6.46 us
  waiting for transfers between devices: 107 us -> 50.6 us
  starting transfers between devices: 29.7 us -> 12.8 us
  blocking collectives: 37 us -> 53.7 us
    dot_general x265 -> x13, matrix products: 394 us -> 5.69 us  [times(): return jnp.einsum('hij,hjv->hiv', a, b, precision=peak_level)]
    another operation x6 -> x1, other arithmetic: 274 us -> 0.03 us  [shards(): edges = jnp.stack([q_in[-RIM:], k_in[-RIM:], v_in[-RIM:]])]
    pallas_call x0 -> x2, Pallas kernels: none -> 134 us  [the longest x1 126 us: local_pass(): pl.pallas_call(local_kernel, grid=(heads // HEADS_PER_STEP,), in_specs=[r...]
    all_to_all x4 -> x0, waiting for transfers between devices: 56 us -> none  [the longest x1 21 us: shards(): lax.all_to_all(v_in, 'head', split_axis=1, concat_axis=0, tiled=True)]
    mul x5 -> x0, local copies, waits for them, and re-layouts: 20.5 us -> none  [the longest x2 10.5 us: unit_rows(): vectors * vectors]
    all_to_all x4 -> x0, starting transfers between devices: 18.9 us -> none  [the longest x1 5.28 us: shards(): lax.all_to_all(v_in, 'head', split_axis=1, concat_axis=0, tiled=True)]
    all_to_all x1 -> x2, blocking collectives: 37 us -> 53.7 us  [the longest x1 29.4 us: incoming_states(): lax.all_to_all(summary, 'head', split_axis=0, concat_axis=0, tiled=True)]
    all_to_all x6 -> x0, local copies, waits for them, and re-layouts: 16.1 us -> none  [the longest x2 6.27 us: shards(): lax.all_to_all(normed, 'head', split_axis=0, concat_axis=1, tiled=True)]
  transfers between devices with their start and end apart: 12 -> 8, of which waited for: 11 -> 8; matrix products, arithmetic and copies ran while one was open for 2% -> 0% of each run, Pallas kernels for 0% -> 0%
where the time goes in v1:
time: 268 us; the launch traced here: 264 us
  Pallas kernels  134 us (50%)
  blocking collectives  53.7 us (20%)
  waiting for transfers between devices  50.6 us (19%)
  starting transfers between devices  12.8 us (5%)
  local copies, waits for them, and re-layouts  6.46 us (2%)
  matrix products  5.69 us (2%)
    pallas_call x1, Pallas kernels, local_pass(): pl.pallas_call(local_kernel, grid=(heads // HEADS_PER_STEP,), in_specs=[r...  126 us
    ppermute x8, waiting for transfers between devices, shifted(): return lax.ppermute(value, axis, [(i, i + 1) for i in range(peers - 1)])  50.6 us
    all_to_all x1, blocking collectives, incoming_states(): lax.all_to_all(summary, 'head', split_axis=0, concat_axis=0, tiled=True)  29.4 us
    all_to_all x1, blocking collectives, incoming_states(): lax.all_to_all(states, 'head', split_axis=0, concat_axis=0, tiled=True)  24.4 us
    ppermute x8, starting transfers between devices, shifted(): return lax.ppermute(value, axis, [(i, i + 1) for i in range(peers - 1)])  12.8 us
    pallas_call x1, Pallas kernels, finish_pass(): pl.pallas_call(finish_kernel, grid=(heads // per,), in_specs=[pl.BlockSpe...  8.41 us
    dot_general x13, matrix products, times(): return jnp.einsum('hij,hjv->hiv', a, b, precision=peak_level)  5.69 us
  transfers between devices with their start and end apart: 8, of which 8 were waited for; matrix products, arithmetic and copies ran while one was open for 0% of the time, Pallas kernels for 0%

profile of v1, /device:TPU:27, one launch (start us, length us, event | category | flops | bytes accessed | tf_op | source)
XLA Modules:
  0.0 263.9 jit_solution(5962504327628301239)
XLA Ops:
  0.0 0.8 slice_bitcast_fusion.5
  0.8 0.9 slice_bitcast_fusion.3
  1.8 3.7 %collective-permute-start = (bf16[3,16,2048]{2,1,0:T(8,128)(2,1)S(1)}, bf16[3,16,2048]{2,1,0:T(8,128)(2,1)S(1)}, u32[]{:S(2)}, u32[]{:S(2)}) collective-permute-start(bf16[3,16,2048]{2,1,0:T(8,128)(2,1)S(1)} %pad_maximum_fusion.1), channel_id=1, source_target_pairs={{0,1},{1,2},{2,3},{3,4},{4,5},{5,6},{6,7},{7,8},{8,9},{9,10},{10,1... | collective-permute-start | bytes 589832 | tf_op jit(solution)/shard_map/ppermute | solution.py:228
  5.5 0.8 copy.10.b_ref
  6.3 1.8 collective-permute-done
  8.1 1.6 copy-done
  12.0 125.7 %local_pass.1 = (f32[16,512,256]{2,1,0:T(8,128)}, f32[16,128,256]{2,1,0:T(8,128)S(1)}) custom-call(bf16[512,2048]{1,0:T(8,128)(2,1)S(1)} %copy-done, bf16[512,2048]{1,0:T(8,128)(2,1)} %k_ref.1, bf16[512,2048]{1,0:T(8,128)(2,1)} %v_ref.1, f32[512,16]{1,0:T(8,128)S(1)} %copy.10.b_ref, bf16[16,2048]{1,0:T(8,128)(2,1)S(1)} %get-tuple-element.47.qr_ref, ...), custom_call_target="tpu_custom_call" | custom-call | tf_op jit(solution)/shard_map/local_pass/pallas_call | solution.py:181
  137.7 29.4 %all_to_all.10 = f32[16,128,256]{2,1,0:T(8,128)S(1)} all-to-all(f32[16,128,256]{2,1,0:T(8,128)S(1)} %get-tuple-element.44), channel_id=1, replica_groups=mesh['seq'=8,'head'=4] {'head'}, dimensions={0} | all-to-all | bytes 4194304 | tf_op jit(solution)/shard_map/all_to_all | solution.py:237
  169.4 1.3 collective-permute-start.1
  170.7 7.3 %collective-permute-done.1 = f32[4,128,128]{2,1,0:T(8,128)S(1)} collective-permute-done((f32[4,128,128]{2,1,0:T(8,128)S(1)}, f32[4,128,128]{2,1,0:T(8,128)S(1)}, u32[]{:S(2)}, u32[]{:S(2)}) %collective-permute-start.1) | collective-permute-done | bytes 262176 | tf_op jit(solution)/shard_map/ppermute | solution.py:228
  178.4 1.3 collective-permute-start.2
  179.7 7.3 %collective-permute-done.2 = f32[4,128,128]{2,1,0:T(8,128)S(1)} collective-permute-done((f32[4,128,128]{2,1,0:T(8,128)S(1)}, f32[4,128,128]{2,1,0:T(8,128)S(1)}, u32[]{:S(2)}, u32[]{:S(2)}) %collective-permute-start.2) | collective-permute-done | bytes 262176 | tf_op jit(solution)/shard_map/ppermute | solution.py:228
  187.4 1.3 collective-permute-start.3
  188.7 6.4 %collective-permute-done.3 = f32[4,128,128]{2,1,0:T(8,128)S(1)} collective-permute-done((f32[4,128,128]{2,1,0:T(8,128)S(1)}, f32[4,128,128]{2,1,0:T(8,128)S(1)}, u32[]{:S(2)}, u32[]{:S(2)}) %collective-permute-start.3) | collective-permute-done | bytes 262176 | tf_op jit(solution)/shard_map/ppermute | solution.py:228
  195.6 1.3 collective-permute-start.4
  196.9 6.7 %collective-permute-done.4 = f32[4,128,128]{2,1,0:T(8,128)S(1)} collective-permute-done((f32[4,128,128]{2,1,0:T(8,128)S(1)}, f32[4,128,128]{2,1,0:T(8,128)S(1)}, u32[]{:S(2)}, u32[]{:S(2)}) %collective-permute-start.4) | collective-permute-done | bytes 262176 | tf_op jit(solution)/shard_map/ppermute | solution.py:228
  204.0 1.3 collective-permute-start.5
  205.3 6.7 %collective-permute-done.5 = f32[4,128,128]{2,1,0:T(8,128)S(1)} collective-permute-done((f32[4,128,128]{2,1,0:T(8,128)S(1)}, f32[4,128,128]{2,1,0:T(8,128)S(1)}, u32[]{:S(2)}, u32[]{:S(2)}) %collective-permute-start.5) | collective-permute-done | bytes 262176 | tf_op jit(solution)/shard_map/ppermute | solution.py:228
  212.4 1.3 collective-permute-start.6
  213.7 6.7 %collective-permute-done.6 = f32[4,128,128]{2,1,0:T(8,128)S(1)} collective-permute-done((f32[4,128,128]{2,1,0:T(8,128)S(1)}, f32[4,128,128]{2,1,0:T(8,128)S(1)}, u32[]{:S(2)}, u32[]{:S(2)}) %collective-permute-start.6) | collective-permute-done | bytes 262176 | tf_op jit(solution)/shard_map/ppermute | solution.py:228
  220.8 1.3 collective-permute-start.7
  222.1 7.6 %collective-permute-done.7 = f32[4,128,128]{2,1,0:T(8,128)S(1)} collective-permute-done((f32[4,128,128]{2,1,0:T(8,128)S(1)}, f32[4,128,128]{2,1,0:T(8,128)S(1)}, u32[]{:S(2)}, u32[]{:S(2)}) %collective-permute-start.7) | collective-permute-done | bytes 262176 | tf_op jit(solution)/shard_map/ppermute | solution.py:228
  231.1 24.4 %all_to_all.11.state_ref = f32[16,128,128]{2,1,0:T(8,128)S(1)} all-to-all(f32[16,128,128]{2,1,0:T(8,128)S(1)} %pad_maximum_fusion), channel_id=1, replica_groups=mesh['seq'=8,'head'=4] {'head'}, dimensions={0} | all-to-all | bytes 2097152 | tf_op jit(solution)/shard_map/all_to_all | solution.py:251
  255.5 8.4 %finish_pass.1 = bf16[512,2048]{1,0:T(8,128)(2,1)} custom-call(f32[16,512,256]{2,1,0:T(8,128)} %get-tuple-element.43.part_ref, f32[16,128,128]{2,1,0:T(8,128)S(1)} %all_to_all.11.state_ref, f32[1,128]{1,0:T(1,128)S(1)} %bitcast.24), custom_call_target="tpu_custom_call" | custom-call | tf_op jit(solution)/shard_map/finish_pass/pallas_call | solution.py:211
  (30 shorter events, 8.3 us)
Async XLA Ops:
  1.8 6.3 %collective-permute-start = (bf16[3,16,2048]{2,1,0:T(8,128)(2,1)S(1)}, bf16[3,16,2048]{2,1,0:T(8,128)(2,1)S(1)}, u32[]{:S(2)}, u32[]{:S(2)}) collective-permute-start(bf16[3,16,2048]{2,1,0:T(8,128)(2,1)S(1)} %pad_maximum_fusion.1), channel_id=1, source_target_pairs={{0,1},{1,2},{2,3},{3,4},{4,5},{5,6},{6,7},{7,8},{8,9},{9,10},{10,1... | collective-permute-start | bytes 589832 | tf_op jit(solution)/shard_map/ppermute | solution.py:228
  8.1 1.6 copy-start
  9.7 0.8 copy-start.1
  10.4 0.8 copy-start.2
  11.2 0.8 copy-start.3
  169.4 8.6 %collective-permute-start.1 = (f32[4,128,128]{2,1,0:T(8,128)S(1)}, f32[4,128,128]{2,1,0:T(8,128)S(1)}, u32[]{:S(2)}, u32[]{:S(2)}) collective-permute-start(f32[4,128,128]{2,1,0:T(8,128)S(1)} %convolution_add_fusion.9), channel_id=1, source_target_pairs={{0,4},{4,8},{8,12},{12,16},{16,20},{20,24},{24,28},{1,5},{5,9},{9,... | collective-permute-start | bytes 786440 | tf_op jit(solution)/shard_map/ppermute | solution.py:228
  178.4 8.6 %collective-permute-start.2 = (f32[4,128,128]{2,1,0:T(8,128)S(1)}, f32[4,128,128]{2,1,0:T(8,128)S(1)}, u32[]{:S(2)}, u32[]{:S(2)}) collective-permute-start(f32[4,128,128]{2,1,0:T(8,128)S(1)} %convolution_add_fusion.8), channel_id=1, source_target_pairs={{0,4},{4,8},{8,12},{12,16},{16,20},{20,24},{24,28},{1,5},{5,9},{9,... | collective-permute-start | bytes 786440 | tf_op jit(solution)/shard_map/ppermute | solution.py:228
  187.4 7.7 %collective-permute-start.3 = (f32[4,128,128]{2,1,0:T(8,128)S(1)}, f32[4,128,128]{2,1,0:T(8,128)S(1)}, u32[]{:S(2)}, u32[]{:S(2)}) collective-permute-start(f32[4,128,128]{2,1,0:T(8,128)S(1)} %convolution_add_fusion.7), channel_id=1, source_target_pairs={{0,4},{4,8},{8,12},{12,16},{16,20},{20,24},{24,28},{1,5},{5,9},{9,... | collective-permute-start | bytes 786440 | tf_op jit(solution)/shard_map/ppermute | solution.py:228
  195.6 8.0 %collective-permute-start.4 = (f32[4,128,128]{2,1,0:T(8,128)S(1)}, f32[4,128,128]{2,1,0:T(8,128)S(1)}, u32[]{:S(2)}, u32[]{:S(2)}) collective-permute-start(f32[4,128,128]{2,1,0:T(8,128)S(1)} %convolution_add_fusion.6), channel_id=1, source_target_pairs={{0,4},{4,8},{8,12},{12,16},{16,20},{20,24},{24,28},{1,5},{5,9},{9,... | collective-permute-start | bytes 786440 | tf_op jit(solution)/shard_map/ppermute | solution.py:228
  204.0 8.0 %collective-permute-start.5 = (f32[4,128,128]{2,1,0:T(8,128)S(1)}, f32[4,128,128]{2,1,0:T(8,128)S(1)}, u32[]{:S(2)}, u32[]{:S(2)}) collective-permute-start(f32[4,128,128]{2,1,0:T(8,128)S(1)} %convolution_add_fusion.5), channel_id=1, source_target_pairs={{0,4},{4,8},{8,12},{12,16},{16,20},{20,24},{24,28},{1,5},{5,9},{9,... | collective-permute-start | bytes 786440 | tf_op jit(solution)/shard_map/ppermute | solution.py:228
  212.4 8.0 %collective-permute-start.6 = (f32[4,128,128]{2,1,0:T(8,128)S(1)}, f32[4,128,128]{2,1,0:T(8,128)S(1)}, u32[]{:S(2)}, u32[]{:S(2)}) collective-permute-start(f32[4,128,128]{2,1,0:T(8,128)S(1)} %convolution_add_fusion.4), channel_id=1, source_target_pairs={{0,4},{4,8},{8,12},{12,16},{16,20},{20,24},{24,28},{1,5},{5,9},{9,... | collective-permute-start | bytes 786440 | tf_op jit(solution)/shard_map/ppermute | solution.py:228
  220.8 8.9 %collective-permute-start.7 = (f32[4,128,128]{2,1,0:T(8,128)S(1)}, f32[4,128,128]{2,1,0:T(8,128)S(1)}, u32[]{:S(2)}, u32[]{:S(2)}) collective-permute-start(f32[4,128,128]{2,1,0:T(8,128)S(1)} %convolution_add_fusion.3), channel_id=1, source_target_pairs={{0,4},{4,8},{8,12},{12,16},{16,20},{20,24},{24,28},{1,5},{5,9},{9,... | collective-permute-start | bytes 786440 | tf_op jit(solution)/shard_map/ppermute | solution.py:228
  231.0 24.5 %copy-start.4 = (f32[128]{0:T(128)S(1)}, f32[128]{0:T(128)}, u32[]{:S(2)}) copy-start(f32[128]{0:T(128)} %param.21) | copy-start | bytes 1540

commit v2 on v1

--- a/solution.py
+++ b/solution.py
@@ -11,7 +11,7 @@
 KW = 4
 RIM = 16
 BASE = 8
-HEADS_PER_STEP = 2
+HEADS_PER_STEP = 4
 
 F32 = jnp.float32
 BF16 = jnp.bfloat16
@@ -62,7 +62,7 @@
     return fold(out)
 
 
-def lower_inverse(g):
+def base_inverse(g):
     lane = lax.broadcasted_iota(jnp.int32, (BASE, CHUNK), 1)
     sub = lax.broadcasted_iota(jnp.int32, (BASE, CHUNK), 0)
     groups = CHUNK // BASE
@@ -77,9 +77,13 @@
         for by in (1, 2, 4):
             column = column + pltpu.roll(column, by, 1)
         x = x - column * jnp.broadcast_to(x[j : j + 1, :], (BASE, CHUNK))
-    inv = jnp.concatenate(
+    return jnp.concatenate(
         [jnp.where(lane // BASE == i, x, 0.0) for i in range(groups)], axis=0
     )
+
+
+def lower_inverses(gs):
+    invs = [base_inverse(g) for g in gs]
     col = lax.broadcasted_iota(jnp.int32, (CHUNK, CHUNK), 1)
     row = lax.broadcasted_iota(jnp.int32, (CHUNK, CHUNK), 0)
     size = BASE
@@ -87,21 +91,30 @@
         pairs = CHUNK // (2 * size)
         low = [slice((2 * p + 1) * size, (2 * p + 2) * size) for p in range(pairs)]
         up = [slice(2 * p * size, (2 * p + 1) * size) for p in range(pairs)]
-        corner = jnp.where(col // size == row // size - 1, g, 0.0)
-        corner = jnp.concatenate([corner[s] for s in low], axis=0)
-        old = jnp.concatenate([inv[s] for s in low], axis=0)
-        e = mm_square(corner, inv)
+        corner_mask = col // size == row // size - 1
         zero = jnp.zeros((size, CHUNK), F32)
-        e_full = jnp.concatenate(
-            [t for p in range(pairs) for t in (zero, e[p * size : (p + 1) * size])], axis=0
-        )
-        new = old - mm_square(old, e_full)
-        inv = jnp.concatenate(
-            [t for p in range(pairs) for t in (inv[up[p]], new[p * size : (p + 1) * size])],
-            axis=0,
-        )
+        olds, products = [], []
+        for g, inv in zip(gs, invs):
+            corner = jnp.where(corner_mask, g, 0.0)
+            corner = jnp.concatenate([corner[s] for s in low], axis=0)
+            olds.append(jnp.concatenate([inv[s] for s in low], axis=0))
+            products.append(mm_square(corner, inv))
+        fulls = [
+            jnp.concatenate(
+                [t for p in range(pairs) for t in (zero, e[p * size : (p + 1) * size])], axis=0
+            )
+            for e in products
+        ]
+        news = [old - mm_square(old, full) for old, full in zip(olds, fulls)]
+        invs = [
+            jnp.concatenate(
+                [t for p in range(pairs) for t in (inv[up[p]], new[p * size : (p + 1) * size])],
+                axis=0,
+            )
+            for inv, new in zip(invs, news)
+        ]
         size *= 2
-    return inv
+    return invs
 
 
 def conv_silu(x_ref, rim_ref, w_ref, pad, lanes):
@@ -129,7 +142,7 @@
     col = lax.broadcasted_iota(jnp.int32, (CHUNK, CHUNK), 1)
     beta = b_ref[...]
     which = lax.broadcasted_iota(jnp.int32, beta.shape, 1)
-    prepared = []
+    chunk_rows, grams, scores = [], [], []
     for i in range(HEADS_PER_STEP):
         lanes = slice(i * WIDTH, (i + 1) * WIDTH)
         q = unit_rows(conv_silu(q_ref, qr_ref, cq_ref, pads[3 * i], lanes))
@@ -137,38 +150,44 @@
         v = conv_silu(v_ref, vr_ref, cv_ref, pads[3 * i + 2], lanes)
         head = step * HEADS_PER_STEP + i
         b = jnp.sum(jnp.where(which == head, beta, 0.0), axis=1, keepdims=True)
-        parts = []
         for n in range(chunks):
             rows = slice(n * CHUNK, (n + 1) * CHUNK)
             qn, kn, vn, bn = q[rows], k[rows], v[rows], b[rows]
             both = gram(jnp.concatenate([qn, kn], axis=0), kn)
             p = jnp.where(row >= col, both[:CHUNK], 0.0)
-            g = jnp.where(row > col, both[CHUNK:] * bn, 0.0)
-            inv = lower_inverse(g)
-            wu = mm_wide(inv, jnp.concatenate([kn * bn, vn * bn], axis=1))
-            parts.append((qn, jnp.concatenate([p, kn.T], axis=0), wu))
-        prepared.append(parts)
+            grams.append(jnp.where(row > col, both[CHUNK:] * bn, 0.0))
+            scores.append(jnp.concatenate([p, kn.T], axis=0))
+            chunk_rows.append((qn, jnp.concatenate([kn * bn, vn * bn], axis=1)))
+    prepared = [
+        (qn, pk, mm_wide(inv, kv))
+        for (qn, kv), pk, inv in zip(chunk_rows, scores, lower_inverses(grams))
+    ]
     zero = jnp.zeros((CHUNK, WIDTH), F32)
-    carried = [None] * HEADS_PER_STEP
     for n in range(chunks):
+        now = [prepared[i * chunks + n] for i in range(HEADS_PER_STEP)]
+        if n == 0:
+            eye = jnp.where(row == col, 1.0, 0.0).astype(F32)
+            states = [jnp.concatenate([eye, zero], axis=1)] * HEADS_PER_STEP
+            fresh = [
+                jnp.concatenate([-wu[:, :WIDTH], wu[:, WIDTH:]], axis=1) for ignored, pk, wu in now
+            ]
+            seen = [jnp.concatenate([qn, zero], axis=1) for qn, pk, wu in now]
+        else:
+            moved = [
+                mm_wide(jnp.concatenate([wu[:, :WIDTH], qn], axis=0), state)
+                for (qn, pk, wu), state in zip(now, states)
+            ]
+            fresh = [
+                jnp.concatenate([zero, wu[:, WIDTH:]], axis=1) - m[:CHUNK]
+                for (qn, pk, wu), m in zip(now, moved)
+            ]
+            seen = [m[CHUNK:] for m in moved]
+        added = [mm_wide(pk, f) for (qn, pk, wu), f in zip(now, fresh)]
         for i in range(HEADS_PER_STEP):
-            qn, pk, wu = prepared[i][n]
-            w, u = wu[:, :WIDTH], wu[:, WIDTH:]
-            if n == 0:
-                fresh = jnp.concatenate([-w, u], axis=1)
-                seen = jnp.concatenate([qn, zero], axis=1)
-                eye = jnp.where(row == col, 1.0, 0.0).astype(F32)
-                state = jnp.concatenate([eye, zero], axis=1)
-            else:
-                state = carried[i]
-                moved = mm_wide(jnp.concatenate([w, qn], axis=0), state)
-                fresh = jnp.concatenate([zero, u], axis=1) - moved[:CHUNK]
-                seen = moved[CHUNK:]
-            added = mm_wide(pk, fresh)
-            out_ref[i, n * CHUNK : (n + 1) * CHUNK, :] = seen + added[:CHUNK]
-            carried[i] = state + added[CHUNK:]
+            out_ref[i, n * CHUNK : (n + 1) * CHUNK, :] = seen[i] + added[i][:CHUNK]
+        states = [state + a[CHUNK:] for state, a in zip(states, added)]
     for i in range(HEADS_PER_STEP):
-        sum_ref[i, :, :] = carried[i]
+        sum_ref[i, :, :] = states[i]
 
 
 def local_pass(q, k, v, beta, rims, conv_q, conv_k, conv_v):

time: 268 us -> 180 us (0.67)
  the two profiles are of different devices: /device:TPU:27 before, /device:TPU:24 now
where the time goes in v2:
time: 180 us; the launch traced here: 179 us
  waiting for transfers between devices  58.7 us (33%)
  Pallas kernels  46.6 us (26%)
  blocking collectives  45 us (25%)
  starting transfers between devices  16.1 us (9%)
  local copies, waits for them, and re-layouts  6.46 us (4%)
  matrix products  5.7 us (3%)
    ppermute x8, waiting for transfers between devices, shifted(): return lax.ppermute(value, axis, [(i, i + 1) for i in range(peers - 1)])  58.7 us
    pallas_call x1, Pallas kernels, local_pass(): pl.pallas_call(local_kernel, grid=(heads // HEADS_PER_STEP,), in_specs=[r...  38.2 us
    all_to_all x1, blocking collectives, incoming_states(): lax.all_to_all(summary, 'head', split_axis=0, concat_axis=0, tiled=True)  28.2 us
    all_to_all x1, blocking collectives, incoming_states(): lax.all_to_all(states, 'head', split_axis=0, concat_axis=0, tiled=True)  16.9 us
    ppermute x8, starting transfers between devices, shifted(): return lax.ppermute(value, axis, [(i, i + 1) for i in range(peers - 1)])  16.1 us
    pallas_call x1, Pallas kernels, finish_pass(): pl.pallas_call(finish_kernel, grid=(heads // per,), in_specs=[pl.BlockSpe...  8.4 us
    dot_general x13, matrix products, times(): return jnp.einsum('hij,hjv->hiv', a, b, precision=peak_level)  5.7 us
    unnamed x10, local copies, waits for them, and re-layouts  3.86 us
  transfers between devices with their start and end apart: 8, of which 8 were waited for; matrix products, arithmetic and copies ran while one was open for 0% of the time, Pallas kernels for 0%

profile of v2, /device:TPU:24, one launch (start us, length us, event | category | flops | bytes accessed | tf_op | source)
XLA Modules:
  0.0 179.1 jit_solution(243010912366732043)
XLA Ops:
  0.0 0.8 slice_bitcast_fusion.5
  0.8 0.9 slice_bitcast_fusion.3
  1.8 1.9 %collective-permute-start = (bf16[3,16,2048]{2,1,0:T(8,128)(2,1)S(1)}, bf16[3,16,2048]{2,1,0:T(8,128)(2,1)S(1)}, u32[]{:S(2)}, u32[]{:S(2)}) collective-permute-start(bf16[3,16,2048]{2,1,0:T(8,128)(2,1)S(1)} %pad_maximum_fusion.1), channel_id=1, source_target_pairs={{0,1},{1,2},{2,3},{3,4},{4,5},{5,6},{6,7},{7,8},{8,9},{9,10},{10,1... | collective-permute-start | bytes 589832 | tf_op jit(solution)/shard_map/ppermute | solution.py:247
  3.7 0.8 copy.10.b_ref
  4.5 6.0 %collective-permute-done = bf16[3,16,2048]{2,1,0:T(8,128)(2,1)S(1)} collective-permute-done((bf16[3,16,2048]{2,1,0:T(8,128)(2,1)S(1)}, bf16[3,16,2048]{2,1,0:T(8,128)(2,1)S(1)}, u32[]{:S(2)}, u32[]{:S(2)}) %collective-permute-start) | collective-permute-done | bytes 196640 | tf_op jit(solution)/shard_map/ppermute | solution.py:247
  10.6 1.6 copy-done
  14.4 38.2 %local_pass.1 = (f32[16,512,256]{2,1,0:T(8,128)}, f32[16,128,256]{2,1,0:T(8,128)S(1)}) custom-call(bf16[512,2048]{1,0:T(8,128)(2,1)S(1)} %copy-done, bf16[512,2048]{1,0:T(8,128)(2,1)} %k_ref.1, bf16[512,2048]{1,0:T(8,128)(2,1)} %v_ref.1, f32[512,16]{1,0:T(8,128)S(1)} %copy.10.b_ref, bf16[16,2048]{1,0:T(8,128)(2,1)S(1)} %get-tuple-element.47.qr_ref, ...), custom_call_target="tpu_custom_call" | custom-call | tf_op jit(solution)/shard_map/local_pass/pallas_call | solution.py:200
  52.6 28.2 %all_to_all.10 = f32[16,128,256]{2,1,0:T(8,128)S(1)} all-to-all(f32[16,128,256]{2,1,0:T(8,128)S(1)} %get-tuple-element.44), channel_id=1, replica_groups=mesh['seq'=8,'head'=4] {'head'}, dimensions={0} | all-to-all | bytes 4194304 | tf_op jit(solution)/shard_map/all_to_all | solution.py:256
  83.1 2.5 %collective-permute-start.1 = (f32[4,128,128]{2,1,0:T(8,128)S(1)}, f32[4,128,128]{2,1,0:T(8,128)S(1)}, u32[]{:S(2)}, u32[]{:S(2)}) collective-permute-start(f32[4,128,128]{2,1,0:T(8,128)S(1)} %convolution_add_fusion.9), channel_id=1, source_target_pairs={{0,4},{4,8},{8,12},{12,16},{16,20},{20,24},{24,28},{1,5},{5,9},{9,... | collective-permute-start | bytes 786440 | tf_op jit(solution)/shard_map/ppermute | solution.py:247
  85.6 8.0 %collective-permute-done.1 = f32[4,128,128]{2,1,0:T(8,128)S(1)} collective-permute-done((f32[4,128,128]{2,1,0:T(8,128)S(1)}, f32[4,128,128]{2,1,0:T(8,128)S(1)}, u32[]{:S(2)}, u32[]{:S(2)}) %collective-permute-start.1) | collective-permute-done | bytes 262176 | tf_op jit(solution)/shard_map/ppermute | solution.py:247
  94.0 1.9 %collective-permute-start.2 = (f32[4,128,128]{2,1,0:T(8,128)S(1)}, f32[4,128,128]{2,1,0:T(8,128)S(1)}, u32[]{:S(2)}, u32[]{:S(2)}) collective-permute-start(f32[4,128,128]{2,1,0:T(8,128)S(1)} %convolution_add_fusion.8), channel_id=1, source_target_pairs={{0,4},{4,8},{8,12},{12,16},{16,20},{20,24},{24,28},{1,5},{5,9},{9,... | collective-permute-start | bytes 786440 | tf_op jit(solution)/shard_map/ppermute | solution.py:247
  95.9 7.6 %collective-permute-done.2 = f32[4,128,128]{2,1,0:T(8,128)S(1)} collective-permute-done((f32[4,128,128]{2,1,0:T(8,128)S(1)}, f32[4,128,128]{2,1,0:T(8,128)S(1)}, u32[]{:S(2)}, u32[]{:S(2)}) %collective-permute-start.2) | collective-permute-done | bytes 262176 | tf_op jit(solution)/shard_map/ppermute | solution.py:247
  103.9 1.9 %collective-permute-start.3 = (f32[4,128,128]{2,1,0:T(8,128)S(1)}, f32[4,128,128]{2,1,0:T(8,128)S(1)}, u32[]{:S(2)}, u32[]{:S(2)}) collective-permute-start(f32[4,128,128]{2,1,0:T(8,128)S(1)} %convolution_add_fusion.7), channel_id=1, source_target_pairs={{0,4},{4,8},{8,12},{12,16},{16,20},{20,24},{24,28},{1,5},{5,9},{9,... | collective-permute-start | bytes 786440 | tf_op jit(solution)/shard_map/ppermute | solution.py:247
  105.9 7.2 %collective-permute-done.3 = f32[4,128,128]{2,1,0:T(8,128)S(1)} collective-permute-done((f32[4,128,128]{2,1,0:T(8,128)S(1)}, f32[4,128,128]{2,1,0:T(8,128)S(1)}, u32[]{:S(2)}, u32[]{:S(2)}) %collective-permute-start.3) | collective-permute-done | bytes 262176 | tf_op jit(solution)/shard_map/ppermute | solution.py:247
  113.5 2.1 %collective-permute-start.4 = (f32[4,128,128]{2,1,0:T(8,128)S(1)}, f32[4,128,128]{2,1,0:T(8,128)S(1)}, u32[]{:S(2)}, u32[]{:S(2)}) collective-permute-start(f32[4,128,128]{2,1,0:T(8,128)S(1)} %convolution_add_fusion.6), channel_id=1, source_target_pairs={{0,4},{4,8},{8,12},{12,16},{16,20},{20,24},{24,28},{1,5},{5,9},{9,... | collective-permute-start | bytes 786440 | tf_op jit(solution)/shard_map/ppermute | solution.py:247
  115.6 7.1 %collective-permute-done.4 = f32[4,128,128]{2,1,0:T(8,128)S(1)} collective-permute-done((f32[4,128,128]{2,1,0:T(8,128)S(1)}, f32[4,128,128]{2,1,0:T(8,128)S(1)}, u32[]{:S(2)}, u32[]{:S(2)}) %collective-permute-start.4) | collective-permute-done | bytes 262176 | tf_op jit(solution)/shard_map/ppermute | solution.py:247
  123.1 1.9 %collective-permute-start.5 = (f32[4,128,128]{2,1,0:T(8,128)S(1)}, f32[4,128,128]{2,1,0:T(8,128)S(1)}, u32[]{:S(2)}, u32[]{:S(2)}) collective-permute-start(f32[4,128,128]{2,1,0:T(8,128)S(1)} %convolution_add_fusion.5), channel_id=1, source_target_pairs={{0,4},{4,8},{8,12},{12,16},{16,20},{20,24},{24,28},{1,5},{5,9},{9,... | collective-permute-start | bytes 786440 | tf_op jit(solution)/shard_map/ppermute | solution.py:247
  125.0 7.2 %collective-permute-done.5 = f32[4,128,128]{2,1,0:T(8,128)S(1)} collective-permute-done((f32[4,128,128]{2,1,0:T(8,128)S(1)}, f32[4,128,128]{2,1,0:T(8,128)S(1)}, u32[]{:S(2)}, u32[]{:S(2)}) %collective-permute-start.5) | collective-permute-done | bytes 262176 | tf_op jit(solution)/shard_map/ppermute | solution.py:247
  132.6 1.9 %collective-permute-start.6 = (f32[4,128,128]{2,1,0:T(8,128)S(1)}, f32[4,128,128]{2,1,0:T(8,128)S(1)}, u32[]{:S(2)}, u32[]{:S(2)}) collective-permute-start(f32[4,128,128]{2,1,0:T(8,128)S(1)} %convolution_add_fusion.4), channel_id=1, source_target_pairs={{0,4},{4,8},{8,12},{12,16},{16,20},{20,24},{24,28},{1,5},{5,9},{9,... | collective-permute-start | bytes 786440 | tf_op jit(solution)/shard_map/ppermute | solution.py:247
  134.6 8.3 %collective-permute-done.6 = f32[4,128,128]{2,1,0:T(8,128)S(1)} collective-permute-done((f32[4,128,128]{2,1,0:T(8,128)S(1)}, f32[4,128,128]{2,1,0:T(8,128)S(1)}, u32[]{:S(2)}, u32[]{:S(2)}) %collective-permute-start.6) | collective-permute-done | bytes 262176 | tf_op jit(solution)/shard_map/ppermute | solution.py:247
  143.3 1.9 %collective-permute-start.7 = (f32[4,128,128]{2,1,0:T(8,128)S(1)}, f32[4,128,128]{2,1,0:T(8,128)S(1)}, u32[]{:S(2)}, u32[]{:S(2)}) collective-permute-start(f32[4,128,128]{2,1,0:T(8,128)S(1)} %convolution_add_fusion.3), channel_id=1, source_target_pairs={{0,4},{4,8},{8,12},{12,16},{16,20},{20,24},{24,28},{1,5},{5,9},{9,... | collective-permute-start | bytes 786440 | tf_op jit(solution)/shard_map/ppermute | solution.py:247
  145.2 7.2 %collective-permute-done.7 = f32[4,128,128]{2,1,0:T(8,128)S(1)} collective-permute-done((f32[4,128,128]{2,1,0:T(8,128)S(1)}, f32[4,128,128]{2,1,0:T(8,128)S(1)}, u32[]{:S(2)}, u32[]{:S(2)}) %collective-permute-start.7) | collective-permute-done | bytes 262176 | tf_op jit(solution)/shard_map/ppermute | solution.py:247
  153.8 16.9 %all_to_all.11.state_ref = f32[16,128,128]{2,1,0:T(8,128)S(1)} all-to-all(f32[16,128,128]{2,1,0:T(8,128)S(1)} %pad_maximum_fusion), channel_id=1, replica_groups=mesh['seq'=8,'head'=4] {'head'}, dimensions={0} | all-to-all | bytes 2097152 | tf_op jit(solution)/shard_map/all_to_all | solution.py:270
  170.7 8.4 %finish_pass.1 = bf16[512,2048]{1,0:T(8,128)(2,1)} custom-call(f32[16,512,256]{2,1,0:T(8,128)} %get-tuple-element.43.part_ref, f32[16,128,128]{2,1,0:T(8,128)S(1)} %all_to_all.11.state_ref, f32[1,128]{1,0:T(1,128)S(1)} %bitcast.24), custom_call_target="tpu_custom_call" | custom-call | tf_op jit(solution)/shard_map/finish_pass/pallas_call | solution.py:230
  (30 shorter events, 8.3 us)
Async XLA Ops:
  1.8 8.8 %collective-permute-start = (bf16[3,16,2048]{2,1,0:T(8,128)(2,1)S(1)}, bf16[3,16,2048]{2,1,0:T(8,128)(2,1)S(1)}, u32[]{:S(2)}, u32[]{:S(2)}) collective-permute-start(bf16[3,16,2048]{2,1,0:T(8,128)(2,1)S(1)} %pad_maximum_fusion.1), channel_id=1, source_target_pairs={{0,1},{1,2},{2,3},{3,4},{4,5},{5,6},{6,7},{7,8},{8,9},{9,10},{10,1... | collective-permute-start | bytes 589832 | tf_op jit(solution)/shard_map/ppermute | solution.py:247
  10.6 1.6 copy-start
  12.2 0.8 copy-start.1
  12.9 0.8 copy-start.2
  13.7 0.8 copy-start.3
  83.1 10.5 %collective-permute-start.1 = (f32[4,128,128]{2,1,0:T(8,128)S(1)}, f32[4,128,128]{2,1,0:T(8,128)S(1)}, u32[]{:S(2)}, u32[]{:S(2)}) collective-permute-start(f32[4,128,128]{2,1,0:T(8,128)S(1)} %convolution_add_fusion.9), channel_id=1, source_target_pairs={{0,4},{4,8},{8,12},{12,16},{16,20},{20,24},{24,28},{1,5},{5,9},{9,... | collective-permute-start | bytes 786440 | tf_op jit(solution)/shard_map/ppermute | solution.py:247
  94.0 9.5 %collective-permute-start.2 = (f32[4,128,128]{2,1,0:T(8,128)S(1)}, f32[4,128,128]{2,1,0:T(8,128)S(1)}, u32[]{:S(2)}, u32[]{:S(2)}) collective-permute-start(f32[4,128,128]{2,1,0:T(8,128)S(1)} %convolution_add_fusion.8), channel_id=1, source_target_pairs={{0,4},{4,8},{8,12},{12,16},{16,20},{20,24},{24,28},{1,5},{5,9},{9,... | collective-permute-start | bytes 786440 | tf_op jit(solution)/shard_map/ppermute | solution.py:247
  103.9 9.2 %collective-permute-start.3 = (f32[4,128,128]{2,1,0:T(8,128)S(1)}, f32[4,128,128]{2,1,0:T(8,128)S(1)}, u32[]{:S(2)}, u32[]{:S(2)}) collective-permute-start(f32[4,128,128]{2,1,0:T(8,128)S(1)} %convolution_add_fusion.7), channel_id=1, source_target_pairs={{0,4},{4,8},{8,12},{12,16},{16,20},{20,24},{24,28},{1,5},{5,9},{9,... | collective-permute-start | bytes 786440 | tf_op jit(solution)/shard_map/ppermute | solution.py:247
  113.5 9.2 %collective-permute-start.4 = (f32[4,128,128]{2,1,0:T(8,128)S(1)}, f32[4,128,128]{2,1,0:T(8,128)S(1)}, u32[]{:S(2)}, u32[]{:S(2)}) collective-permute-start(f32[4,128,128]{2,1,0:T(8,128)S(1)} %convolution_add_fusion.6), channel_id=1, source_target_pairs={{0,4},{4,8},{8,12},{12,16},{16,20},{20,24},{24,28},{1,5},{5,9},{9,... | collective-permute-start | bytes 786440 | tf_op jit(solution)/shard_map/ppermute | solution.py:247
  123.1 9.2 %collective-permute-start.5 = (f32[4,128,128]{2,1,0:T(8,128)S(1)}, f32[4,128,128]{2,1,0:T(8,128)S(1)}, u32[]{:S(2)}, u32[]{:S(2)}) collective-permute-start(f32[4,128,128]{2,1,0:T(8,128)S(1)} %convolution_add_fusion.5), channel_id=1, source_target_pairs={{0,4},{4,8},{8,12},{12,16},{16,20},{20,24},{24,28},{1,5},{5,9},{9,... | collective-permute-start | bytes 786440 | tf_op jit(solution)/shard_map/ppermute | solution.py:247
  132.6 10.2 %collective-permute-start.6 = (f32[4,128,128]{2,1,0:T(8,128)S(1)}, f32[4,128,128]{2,1,0:T(8,128)S(1)}, u32[]{:S(2)}, u32[]{:S(2)}) collective-permute-start(f32[4,128,128]{2,1,0:T(8,128)S(1)} %convolution_add_fusion.4), channel_id=1, source_target_pairs={{0,4},{4,8},{8,12},{12,16},{16,20},{20,24},{24,28},{1,5},{5,9},{9,... | collective-permute-start | bytes 786440 | tf_op jit(solution)/shard_map/ppermute | solution.py:247
  143.3 9.2 %collective-permute-start.7 = (f32[4,128,128]{2,1,0:T(8,128)S(1)}, f32[4,128,128]{2,1,0:T(8,128)S(1)}, u32[]{:S(2)}, u32[]{:S(2)}) collective-permute-start(f32[4,128,128]{2,1,0:T(8,128)S(1)} %convolution_add_fusion.3), channel_id=1, source_target_pairs={{0,4},{4,8},{8,12},{12,16},{16,20},{20,24},{24,28},{1,5},{5,9},{9,... | collective-permute-start | bytes 786440 | tf_op jit(solution)/shard_map/ppermute | solution.py:247
  153.7 17.0 %copy-start.4 = (f32[128]{0:T(128)S(1)}, f32[128]{0:T(128)}, u32[]{:S(2)}) copy-start(f32[128]{0:T(128)} %param.21) | copy-start | bytes 1540

commit v3 on v2

--- a/solution.py
+++ b/solution.py
@@ -1,4 +1,3 @@
-import functools
 import jax
 import jax.numpy as jnp
 from jax import lax
@@ -15,7 +14,7 @@
 
 F32 = jnp.float32
 BF16 = jnp.bfloat16
-peak_level = lax.Precision.HIGHEST
+MESH = pl.DeviceIdType.MESH
 
 
 def split(x):
@@ -247,27 +246,129 @@
     return lax.ppermute(value, axis, [(i, i + 1) for i in range(peers - 1)])
 
 
-def times(a, b):
-    return jnp.einsum("hij,hjv->hiv", a, b, precision=peak_level)
+def exchange_kernel(sum_ref, state_ref, held, pre, chained, leaving, outgoing,
+                    give_send, give_recv, chain_send, chain_recv, back_send, back_recv):
+    group, local = held.shape[0], held.shape[1]
+    me, place = lax.axis_index("head"), lax.axis_index("seq")
+    length = lax.axis_size("seq")
+    peers = [lax.rem(me + d, group) for d in range(group)]
+    later, earlier = lax.rem(place + 1, length), lax.rem(place + length - 1, length)
+
+    barrier = pltpu.get_barrier_semaphore()
+    for peer in peers[1:]:
+        pl.semaphore_signal(barrier, inc=1, device_id={"head": peer}, device_id_type=MESH)
+    for side in (later, earlier):
+        pl.semaphore_signal(barrier, inc=1, device_id={"seq": side}, device_id_type=MESH)
+    pl.semaphore_wait(barrier, group + 1)
+
+    def give(d, j):
+        return pltpu.make_async_remote_copy(
+            src_ref=sum_ref.at[peers[d] * local + j],
+            dst_ref=held.at[me, j],
+            send_sem=give_send.at[d - 1, j],
+            recv_sem=give_recv.at[d - 1, j],
+            device_id={"head": peers[d]},
+            device_id_type=MESH,
+        )
+
+    def back(d, j):
+        return pltpu.make_async_remote_copy(
+            src_ref=outgoing.at[peers[d], j],
+            dst_ref=state_ref.at[me * local + j],
+            send_sem=back_send.at[d - 1, j],
+            recv_sem=back_recv.at[d - 1, j],
+            device_id={"head": peers[d]},
+            device_id_type=MESH,
+        )
+
+    def chain(j):
+        return pltpu.make_async_remote_copy(
+            src_ref=leaving.at[j],
+            dst_ref=chained.at[j],
+            send_sem=chain_send.at[j],
+            recv_sem=chain_recv.at[j],
+            device_id={"seq": later},
+            device_id_type=MESH,
+        )
+
+    @pl.loop(0, local)
+    def _(j):
+        for d in range(1, group):
+            give(d, j).start()
+
+    @pl.loop(0, local)
+    def _(j):
+        held[me, j] = sum_ref[me * local + j]
+        for d in range(1, group):
+            give(d, j).wait_recv()
+        total = held[0, j]
+        for c in range(1, group):
+            pre[c] = total
+            step = held[c, j]
+            total = mm_wide(step[:, :WIDTH], total)
+            total = jnp.concatenate(
+                [total[:, :WIDTH], total[:, WIDTH:] + step[:, WIDTH:]], axis=1
+            )
+
+        @pl.when(place == 0)
+        def _():
+            chained[j] = jnp.zeros((WIDTH, WIDTH), F32)
+
+        @pl.when(place > 0)
+        def _():
+            chain(j).wait_recv()
+
+        arrived = chained[j]
+        leaving[j] = mm_square(total[:, :WIDTH], arrived) + total[:, WIDTH:]
+
+        @pl.when(place < length - 1)
+        def _():
+            chain(j).start()
+
+        outgoing[0, j] = arrived
+        for c in range(1, group):
+            before = pre[c]
+            outgoing[c, j] = mm_square(before[:, :WIDTH], arrived) + before[:, WIDTH:]
+        for d in range(1, group):
+            back(d, j).start()
+        state_ref[me * local + j] = outgoing[me, j]
+
+    @pl.loop(0, local)
+    def _(j):
+        for d in range(1, group):
+            give(d, j).wait_send()
+            back(d, j).wait()
+
+        @pl.when(place < length - 1)
+        def _():
+            chain(j).wait_send()
 
 
 def incoming_states(summary):
     group = lax.axis_size("head")
-    held = lax.all_to_all(summary, "head", split_axis=0, concat_axis=0, tiled=True)
-    held = held.reshape(group, -1, WIDTH, 2 * WIDTH)
-    before = [None, held[0]]
-    for c in range(1, group):
-        moved = times(held[c][:, :, :WIDTH], before[-1])
-        before.append(moved.at[:, :, WIDTH:].add(held[c][:, :, WIDTH:]))
-    transfer, local = before[-1][:, :, :WIDTH], before[-1][:, :, WIDTH:]
-    arrived = jnp.zeros_like(local)
-    for ignored in range(lax.axis_size("seq") - 1):
-        arrived = shifted(times(transfer, arrived) + local, "seq")
-    states = [arrived]
-    for c in range(1, group):
-        states.append(times(before[c][:, :, :WIDTH], arrived) + before[c][:, :, WIDTH:])
-    states = jnp.concatenate(states, axis=0)
-    return lax.all_to_all(states, "head", split_axis=0, concat_axis=0, tiled=True)
+    heads = summary.shape[0]
+    local = heads // group
+    square = (WIDTH, WIDTH)
+    pairs = pltpu.SemaphoreType.DMA((group - 1, local))
+    singles = pltpu.SemaphoreType.DMA((local,))
+    return pl.pallas_call(
+        exchange_kernel,
+        in_specs=[pl.BlockSpec(memory_space=pltpu.VMEM)],
+        out_specs=pl.BlockSpec(memory_space=pltpu.VMEM),
+        out_shape=jax.ShapeDtypeStruct((heads,) + square, F32),
+        scratch_shapes=[
+            pltpu.VMEM((group, local, WIDTH, 2 * WIDTH), F32),
+            pltpu.VMEM((group, WIDTH, 2 * WIDTH), F32),
+            pltpu.VMEM((local,) + square, F32),
+            pltpu.VMEM((local,) + square, F32),
+            pltpu.VMEM((group, local) + square, F32),
+            pairs, pairs, singles, singles, pairs, pairs,
+        ],
+        compiler_params=pltpu.CompilerParams(
+            collective_id=0, has_side_effects=True, vmem_limit_bytes=32 * 2**20
+        ),
+        name="exchange",
+    )(summary)
 
 
 def shards(q_in, k_in, v_in, beta, conv_q, conv_k, conv_v, out_gain):

time: 180 us -> 117 us (0.65)
  the two profiles are of different devices: /device:TPU:24 before, /device:TPU:27 now
where the time goes in v3:
time: 117 us; the launch traced here: 116 us
  Pallas kernels  104 us (89%)
  local copies, waits for them, and re-layouts  6.42 us (5%)
  starting transfers between devices  3.71 us (3%)
  waiting for transfers between devices  1.77 us (2%)
    pallas_call x1, Pallas kernels, incoming_states(): pl.pallas_call(exchange_kernel, in_specs=[pl.BlockSpec(memory_space=pltpu...  57.6 us
    pallas_call x1, Pallas kernels, local_pass(): pl.pallas_call(local_kernel, grid=(heads // HEADS_PER_STEP,), in_specs=[r...  38.2 us
    pallas_call x1, Pallas kernels, finish_pass(): pl.pallas_call(finish_kernel, grid=(heads // per,), in_specs=[pl.BlockSpe...  8.41 us
    unnamed x10, local copies, waits for them, and re-layouts  3.86 us
    ppermute x1, starting transfers between devices, shifted(): return lax.ppermute(value, axis, [(i, i + 1) for i in range(peers - 1)])  3.71 us
  transfers between devices with their start and end apart: 1, of which 1 were waited for; matrix products, arithmetic and copies ran while one was open for 1% of the time, Pallas kernels for 0%

profile of v3, /device:TPU:27, one launch (start us, length us, event | category | flops | bytes accessed | tf_op | source)
XLA Modules:
  0.0 116.2 jit_solution(13190935765978829107)
XLA Ops:
  0.0 0.8 slice_bitcast_fusion.5
  0.8 0.9 slice_bitcast_fusion.3
  1.8 3.7 %collective-permute-start = (bf16[3,16,2048]{2,1,0:T(8,128)(2,1)S(1)}, bf16[3,16,2048]{2,1,0:T(8,128)(2,1)S(1)}, u32[]{:S(2)}, u32[]{:S(2)}) collective-permute-start(bf16[3,16,2048]{2,1,0:T(8,128)(2,1)S(1)} %pad_maximum_fusion), channel_id=1, source_target_pairs={{0,1},{1,2},{2,3},{3,4},{4,5},{5,6},{6,7},{7,8},{8,9},{9,10},{10,1... | collective-permute-start | bytes 589832 | tf_op jit(solution)/shard_map/ppermute | solution.py:246
  5.5 0.8 copy.10.b_ref
  6.3 1.8 %collective-permute-done = bf16[3,16,2048]{2,1,0:T(8,128)(2,1)S(1)} collective-permute-done((bf16[3,16,2048]{2,1,0:T(8,128)(2,1)S(1)}, bf16[3,16,2048]{2,1,0:T(8,128)(2,1)S(1)}, u32[]{:S(2)}, u32[]{:S(2)}) %collective-permute-start) | collective-permute-done | bytes 196640 | tf_op jit(solution)/shard_map/ppermute | solution.py:246
  8.1 0.0 copy-start
  8.1 1.6 %copy-done = bf16[512,2048]{1,0:T(8,128)(2,1)S(1)} copy-done((bf16[512,2048]{1,0:T(8,128)(2,1)S(1)}, bf16[512,2048]{1,0:T(8,128)(2,1)}, u32[]{:S(2)}) %copy-start) | copy-done | bytes 2097176
  9.7 0.0 copy-start.1
  9.7 0.8 copy-done.1
  10.4 0.0 copy-start.2
  10.4 0.8 copy-done.2
  11.2 0.0 copy-start.3
  11.2 0.8 copy-done.3
  12.0 38.2 %local_pass.1 = (f32[16,512,256]{2,1,0:T(8,128)}, f32[16,128,256]{2,1,0:T(8,128)S(1)}) custom-call(bf16[512,2048]{1,0:T(8,128)(2,1)S(1)} %copy-done, bf16[512,2048]{1,0:T(8,128)(2,1)} %k_ref.1, bf16[512,2048]{1,0:T(8,128)(2,1)} %v_ref.1, f32[512,16]{1,0:T(8,128)S(1)} %copy.10.b_ref, bf16[16,2048]{1,0:T(8,128)(2,1)S(1)} %get-tuple-element.11.qr_ref, ...), custom_call_target="tpu_custom_call" | custom-call | tf_op jit(solution)/shard_map/local_pass/pallas_call | solution.py:199
  50.2 0.0 copy-start.4
  50.2 57.6 %exchange.1.state_ref = f32[16,128,128]{2,1,0:T(8,128)S(1)} custom-call(f32[16,128,256]{2,1,0:T(8,128)S(1)} %get-tuple-element.8.sum_ref), custom_call_target="tpu_custom_call" | custom-call | tf_op jit(solution)/shard_map/exchange/pallas_call | solution.py:354
  107.8 0.0 copy-done.4
  107.8 8.4 %finish_pass.1 = bf16[512,2048]{1,0:T(8,128)(2,1)} custom-call(f32[16,512,256]{2,1,0:T(8,128)} %get-tuple-element.7.part_ref, f32[16,128,128]{2,1,0:T(8,128)S(1)} %exchange.1.state_ref, f32[1,128]{1,0:T(1,128)S(1)} %bitcast.13), custom_call_target="tpu_custom_call" | custom-call | tf_op jit(solution)/shard_map/finish_pass/pallas_call | solution.py:229
  (2 shorter events, 0.0 us)
Async XLA Ops:
  1.8 6.3 %collective-permute-start = (bf16[3,16,2048]{2,1,0:T(8,128)(2,1)S(1)}, bf16[3,16,2048]{2,1,0:T(8,128)(2,1)S(1)}, u32[]{:S(2)}, u32[]{:S(2)}) collective-permute-start(bf16[3,16,2048]{2,1,0:T(8,128)(2,1)S(1)} %pad_maximum_fusion), channel_id=1, source_target_pairs={{0,1},{1,2},{2,3},{3,4},{4,5},{5,6},{6,7},{7,8},{8,9},{9,10},{10,1... | collective-permute-start | bytes 589832 | tf_op jit(solution)/shard_map/ppermute | solution.py:246
  8.1 1.6 %copy-start = (bf16[512,2048]{1,0:T(8,128)(2,1)S(1)}, bf16[512,2048]{1,0:T(8,128)(2,1)}, u32[]{:S(2)}) copy-start(bf16[512,2048]{1,0:T(8,128)(2,1)} %q_ref.1) | copy-start | bytes 6291460
  9.7 0.8 copy-start.1
  10.4 0.8 copy-start.2
  11.2 0.8 copy-start.3
  50.2 57.6 %copy-start.4 = (f32[128]{0:T(128)S(1)}, f32[128]{0:T(128)}, u32[]{:S(2)}) copy-start(f32[128]{0:T(128)} %param.15) | copy-start | bytes 1540

commit v4 on v3

--- a/solution.py
+++ b/solution.py
@@ -210,7 +210,7 @@
             jax.ShapeDtypeStruct((heads, WIDTH, 2 * WIDTH), F32),
         ],
         scratch_shapes=[pltpu.VMEM((RIM + length, WIDTH), F32)] * (3 * HEADS_PER_STEP),
-        compiler_params=pltpu.CompilerParams(vmem_limit_bytes=48 * 2**20),
+        compiler_params=pltpu.CompilerParams(vmem_limit_bytes=60 * 2**20),
         name="local_pass",
     )(q, k, v, beta, *rims, conv_q, conv_k, conv_v)
 
@@ -225,7 +225,7 @@
 
 def finish_pass(parts, states, gain):
     heads, length, ignored = parts.shape
-    per = 2
+    per = 4
     return pl.pallas_call(
         finish_kernel,
         grid=(heads // per,),
@@ -236,7 +236,7 @@
         ],
         out_specs=pl.BlockSpec((length, per * WIDTH), lambda h: (0, h)),
         out_shape=jax.ShapeDtypeStruct((length, heads * WIDTH), BF16),
-        compiler_params=pltpu.CompilerParams(vmem_limit_bytes=48 * 2**20),
+        compiler_params=pltpu.CompilerParams(vmem_limit_bytes=24 * 2**20),
         name="finish_pass",
     )(parts, states, gain.reshape(1, WIDTH))
 
@@ -291,16 +291,20 @@
             device_id_type=MESH,
         )
 
-    @pl.loop(0, local)
-    def _(j):
-        for d in range(1, group):
-            give(d, j).start()
+    for d in range(1, group):
+        give(d, 0).start()
 
     @pl.loop(0, local)
     def _(j):
         held[me, j] = sum_ref[me * local + j]
         for d in range(1, group):
             give(d, j).wait_recv()
+
+        @pl.when(j < local - 1)
+        def _():
+            for d in range(1, group):
+                give(d, j + 1).start()
+
         total = held[0, j]
         for c in range(1, group):
             pre[c] = total
@@ -365,7 +369,7 @@
             pairs, pairs, singles, singles, pairs, pairs,
         ],
         compiler_params=pltpu.CompilerParams(
-            collective_id=0, has_side_effects=True, vmem_limit_bytes=32 * 2**20
+            collective_id=0, has_side_effects=True, vmem_limit_bytes=20 * 2**20
         ),
         name="exchange",
     )(summary)

time: 117 us -> 118 us (level)
  local copies, waits for them, and re-layouts: 6.42 us -> 8.94 us
    pallas_call x1, Pallas kernels: 8.41 us -> 3.33 us  [finish_pass(): pl.pallas_call(finish_kernel, grid=(heads // per,), in_specs=[pl.BlockSpe...]
    pallas_call x1, Pallas kernels: 57.6 us -> 61.6 us  [incoming_states(): pl.pallas_call(exchange_kernel, in_specs=[pl.BlockSpec(memory_space=pltpu...]
    unnamed x10 -> x6, local copies, waits for them, and re-layouts: 3.86 us -> 4.97 us
where the time goes in v4:
time: 118 us
  Pallas kernels  104 us (88%)
  local copies, waits for them, and re-layouts  8.94 us (8%)
  starting transfers between devices  3.71 us (3%)
    pallas_call x1, Pallas kernels, incoming_states(): pl.pallas_call(exchange_kernel, in_specs=[pl.BlockSpec(memory_space=pltpu...  61.6 us
    pallas_call x1, Pallas kernels, local_pass(): pl.pallas_call(local_kernel, grid=(heads // HEADS_PER_STEP,), in_specs=[r...  38.9 us
    unnamed x6, local copies, waits for them, and re-layouts  4.97 us
    ppermute x1, starting transfers between devices, shifted(): return lax.ppermute(value, axis, [(i, i + 1) for i in range(peers - 1)])  3.71 us
    pallas_call x1, Pallas kernels, finish_pass(): pl.pallas_call(finish_kernel, grid=(heads // per,), in_specs=[pl.BlockSpe...  3.33 us
  transfers between devices with their start and end apart: 1, of which 1 were waited for; matrix products, arithmetic and copies ran while one was open for 1% of the time, Pallas kernels for 0%

profile of v4, /device:TPU:27, one launch (start us, length us, event | category | flops | bytes accessed | tf_op | source)
XLA Modules:
  0.0 117.5 jit_solution(6521309216367602346)
XLA Ops:
  0.0 0.8 slice_bitcast_fusion.5
  0.8 0.9 slice_bitcast_fusion.3
  1.8 3.7 %collective-permute-start = (bf16[3,16,2048]{2,1,0:T(8,128)(2,1)S(1)}, bf16[3,16,2048]{2,1,0:T(8,128)(2,1)S(1)}, u32[]{:S(2)}, u32[]{:S(2)}) collective-permute-start(bf16[3,16,2048]{2,1,0:T(8,128)(2,1)S(1)} %pad_maximum_fusion), channel_id=1, source_target_pairs={{0,1},{1,2},{2,3},{3,4},{4,5},{5,6},{6,7},{7,8},{8,9},{9,10},{10,1... | collective-permute-start | bytes 589832 | tf_op jit(solution)/shard_map/ppermute | solution.py:246
  5.5 1.5 %copy.10.b_ref = f32[512,16]{1,0:T(8,128)} copy(bf16[512,16]{0,1:T(8,128)(2,1)} %param.11) | data formatting | bytes 49152 | tf_op jit(solution)/shard_map/convert_element_type | solution.py:382
  7.0 1.0 collective-permute-done
  8.1 0.7 slice_bitcast_fusion
  8.8 38.9 %local_pass.1 = (f32[16,512,256]{2,1,0:T(8,128)}, f32[16,128,256]{2,1,0:T(8,128)}) custom-call(bf16[512,2048]{1,0:T(8,128)(2,1)} %q_ref.1, bf16[512,2048]{1,0:T(8,128)(2,1)} %k_ref.1, bf16[512,2048]{1,0:T(8,128)(2,1)} %v_ref.1, f32[512,16]{1,0:T(8,128)} %copy.10.b_ref, bf16[16,2048]{1,0:T(8,128)(2,1)} %get-tuple-element.11.qr_ref, ...), custom_call_target="tpu_custom_call" | custom-call | tf_op jit(solution)/shard_map/local_pass/pallas_call | solution.py:199
  47.6 0.0 copy-start.2
  47.6 0.0 copy-start.1
  47.6 1.6 %copy-done.1 = f32[16,128,256]{2,1,0:T(8,128)S(1)} copy-done((f32[16,128,256]{2,1,0:T(8,128)S(1)}, f32[16,128,256]{2,1,0:T(8,128)}, u32[]{:S(2)}) %copy-start.1) | copy-done | bytes 2097176
  49.2 61.6 %exchange.1.state_ref = f32[16,128,128]{2,1,0:T(8,128)S(1)} custom-call(f32[16,128,256]{2,1,0:T(8,128)S(1)} %copy-done.1), custom_call_target="tpu_custom_call" | custom-call | tf_op jit(solution)/shard_map/exchange/pallas_call | solution.py:358
  110.8 0.0 copy-done.2
  110.8 0.0 copy-start
  110.8 3.4 %copy-done = f32[16,512,256]{2,1,0:T(8,128)S(1)} copy-done((f32[16,512,256]{2,1,0:T(8,128)S(1)}, f32[16,512,256]{2,1,0:T(8,128)}, u32[]{:S(2)}) %copy-start) | copy-done | bytes 8388632
  114.2 3.3 %finish_pass.1 = bf16[512,2048]{1,0:T(8,128)(2,1)} custom-call(f32[16,512,256]{2,1,0:T(8,128)S(1)} %copy-done, f32[16,128,128]{2,1,0:T(8,128)S(1)} %exchange.1.state_ref, f32[1,128]{1,0:T(1,128)S(1)} %bitcast.13), custom_call_target="tpu_custom_call" | custom-call | tf_op jit(solution)/shard_map/finish_pass/pallas_call | solution.py:229
  (1 shorter events, 0.0 us)
Async XLA Ops:
  1.8 6.3 %collective-permute-start = (bf16[3,16,2048]{2,1,0:T(8,128)(2,1)S(1)}, bf16[3,16,2048]{2,1,0:T(8,128)(2,1)S(1)}, u32[]{:S(2)}, u32[]{:S(2)}) collective-permute-start(bf16[3,16,2048]{2,1,0:T(8,128)(2,1)S(1)} %pad_maximum_fusion), channel_id=1, source_target_pairs={{0,1},{1,2},{2,3},{3,4},{4,5},{5,6},{6,7},{7,8},{8,9},{9,10},{10,1... | collective-permute-start | bytes 589832 | tf_op jit(solution)/shard_map/ppermute | solution.py:246
  47.6 63.2 %copy-start.2 = (f32[128]{0:T(128)S(1)}, f32[128]{0:T(128)}, u32[]{:S(2)}) copy-start(f32[128]{0:T(128)} %param.15) | copy-start | bytes 1540
  47.6 1.6 %copy-start.1 = (f32[16,128,256]{2,1,0:T(8,128)S(1)}, f32[16,128,256]{2,1,0:T(8,128)}, u32[]{:S(2)}) copy-start(f32[16,128,256]{2,1,0:T(8,128)} %get-tuple-element.8.sum_ref) | copy-start | bytes 6291460
  110.8 3.4 %copy-start = (f32[16,512,256]{2,1,0:T(8,128)S(1)}, f32[16,512,256]{2,1,0:T(8,128)}, u32[]{:S(2)}) copy-start(f32[16,512,256]{2,1,0:T(8,128)} %get-tuple-element.7.part_ref) | copy-start | bytes 25165828

commit v5 on v3

--- a/solution.py
+++ b/solution.py
@@ -210,7 +210,7 @@
             jax.ShapeDtypeStruct((heads, WIDTH, 2 * WIDTH), F32),
         ],
         scratch_shapes=[pltpu.VMEM((RIM + length, WIDTH), F32)] * (3 * HEADS_PER_STEP),
-        compiler_params=pltpu.CompilerParams(vmem_limit_bytes=48 * 2**20),
+        compiler_params=pltpu.CompilerParams(vmem_limit_bytes=60 * 2**20),
         name="local_pass",
     )(q, k, v, beta, *rims, conv_q, conv_k, conv_v)
 
@@ -225,7 +225,7 @@
 
 def finish_pass(parts, states, gain):
     heads, length, ignored = parts.shape
-    per = 2
+    per = 4
     return pl.pallas_call(
         finish_kernel,
         grid=(heads // per,),
@@ -236,7 +236,7 @@
         ],
         out_specs=pl.BlockSpec((length, per * WIDTH), lambda h: (0, h)),
         out_shape=jax.ShapeDtypeStruct((length, heads * WIDTH), BF16),
-        compiler_params=pltpu.CompilerParams(vmem_limit_bytes=48 * 2**20),
+        compiler_params=pltpu.CompilerParams(vmem_limit_bytes=24 * 2**20),
         name="finish_pass",
     )(parts, states, gain.reshape(1, WIDTH))
 
@@ -365,7 +365,7 @@
             pairs, pairs, singles, singles, pairs, pairs,
         ],
         compiler_params=pltpu.CompilerParams(
-            collective_id=0, has_side_effects=True, vmem_limit_bytes=32 * 2**20
+            collective_id=0, has_side_effects=True, vmem_limit_bytes=20 * 2**20
         ),
         name="exchange",
     )(summary)

time: 117 us -> 114 us (0.974)
  Pallas kernels: 104 us -> 99.8 us
  local copies, waits for them, and re-layouts: 6.42 us -> 8.94 us
    pallas_call x1, Pallas kernels: 8.41 us -> 3.33 us  [finish_pass(): pl.pallas_call(finish_kernel, grid=(heads // per,), in_specs=[pl.BlockSpe...]
    unnamed x10 -> x6, local copies, waits for them, and re-layouts: 3.86 us -> 4.97 us
where the time goes in v5:
time: 114 us
  Pallas kernels  99.8 us (88%)
  local copies, waits for them, and re-layouts  8.94 us (8%)
  starting transfers between devices  3.71 us (3%)
    pallas_call x1, Pallas kernels, incoming_states(): pl.pallas_call(exchange_kernel, in_specs=[pl.BlockSpec(memory_space=pltpu...  57.6 us
    pallas_call x1, Pallas kernels, local_pass(): pl.pallas_call(local_kernel, grid=(heads // HEADS_PER_STEP,), in_specs=[r...  38.9 us
    unnamed x6, local copies, waits for them, and re-layouts  4.97 us
    ppermute x1, starting transfers between devices, shifted(): return lax.ppermute(value, axis, [(i, i + 1) for i in range(peers - 1)])  3.71 us
    pallas_call x1, Pallas kernels, finish_pass(): pl.pallas_call(finish_kernel, grid=(heads // per,), in_specs=[pl.BlockSpe...  3.33 us
  transfers between devices with their start and end apart: 1, of which 1 were waited for; matrix products, arithmetic and copies ran while one was open for 1% of the time, Pallas kernels for 0%

profile of v5, /device:TPU:27, one launch (start us, length us, event | category | flops | bytes accessed | tf_op | source)
XLA Modules:
  0.0 113.6 jit_solution(434167460464745216)
XLA Ops:
  0.0 0.8 slice_bitcast_fusion.5
  0.8 0.9 slice_bitcast_fusion.3
  1.8 3.7 %collective-permute-start = (bf16[3,16,2048]{2,1,0:T(8,128)(2,1)S(1)}, bf16[3,16,2048]{2,1,0:T(8,128)(2,1)S(1)}, u32[]{:S(2)}, u32[]{:S(2)}) collective-permute-start(bf16[3,16,2048]{2,1,0:T(8,128)(2,1)S(1)} %pad_maximum_fusion), channel_id=1, source_target_pairs={{0,1},{1,2},{2,3},{3,4},{4,5},{5,6},{6,7},{7,8},{8,9},{9,10},{10,1... | collective-permute-start | bytes 589832 | tf_op jit(solution)/shard_map/ppermute | solution.py:246
  5.5 1.5 %copy.10.b_ref = f32[512,16]{1,0:T(8,128)} copy(bf16[512,16]{0,1:T(8,128)(2,1)} %param.11) | data formatting | bytes 49152 | tf_op jit(solution)/shard_map/convert_element_type | solution.py:378
  7.0 1.0 collective-permute-done
  8.1 0.7 slice_bitcast_fusion
  8.8 38.9 %local_pass.1 = (f32[16,512,256]{2,1,0:T(8,128)}, f32[16,128,256]{2,1,0:T(8,128)}) custom-call(bf16[512,2048]{1,0:T(8,128)(2,1)} %q_ref.1, bf16[512,2048]{1,0:T(8,128)(2,1)} %k_ref.1, bf16[512,2048]{1,0:T(8,128)(2,1)} %v_ref.1, f32[512,16]{1,0:T(8,128)} %copy.10.b_ref, bf16[16,2048]{1,0:T(8,128)(2,1)} %get-tuple-element.11.qr_ref, ...), custom_call_target="tpu_custom_call" | custom-call | tf_op jit(solution)/shard_map/local_pass/pallas_call | solution.py:199
  47.6 0.0 copy-start.2
  47.6 0.0 copy-start.1
  47.6 1.6 %copy-done.1 = f32[16,128,256]{2,1,0:T(8,128)S(1)} copy-done((f32[16,128,256]{2,1,0:T(8,128)S(1)}, f32[16,128,256]{2,1,0:T(8,128)}, u32[]{:S(2)}) %copy-start.1) | copy-done | bytes 2097176
  49.2 57.6 %exchange.1.state_ref = f32[16,128,128]{2,1,0:T(8,128)S(1)} custom-call(f32[16,128,256]{2,1,0:T(8,128)S(1)} %copy-done.1), custom_call_target="tpu_custom_call" | custom-call | tf_op jit(solution)/shard_map/exchange/pallas_call | solution.py:354
  106.8 0.0 copy-done.2
  106.9 0.0 copy-start
  106.9 3.4 %copy-done = f32[16,512,256]{2,1,0:T(8,128)S(1)} copy-done((f32[16,512,256]{2,1,0:T(8,128)S(1)}, f32[16,512,256]{2,1,0:T(8,128)}, u32[]{:S(2)}) %copy-start) | copy-done | bytes 8388632
  110.2 3.3 %finish_pass.1 = bf16[512,2048]{1,0:T(8,128)(2,1)} custom-call(f32[16,512,256]{2,1,0:T(8,128)S(1)} %copy-done, f32[16,128,128]{2,1,0:T(8,128)S(1)} %exchange.1.state_ref, f32[1,128]{1,0:T(1,128)S(1)} %bitcast.13), custom_call_target="tpu_custom_call" | custom-call | tf_op jit(solution)/shard_map/finish_pass/pallas_call | solution.py:229
  (1 shorter events, 0.0 us)
Async XLA Ops:
  1.8 6.3 %collective-permute-start = (bf16[3,16,2048]{2,1,0:T(8,128)(2,1)S(1)}, bf16[3,16,2048]{2,1,0:T(8,128)(2,1)S(1)}, u32[]{:S(2)}, u32[]{:S(2)}) collective-permute-start(bf16[3,16,2048]{2,1,0:T(8,128)(2,1)S(1)} %pad_maximum_fusion), channel_id=1, source_target_pairs={{0,1},{1,2},{2,3},{3,4},{4,5},{5,6},{6,7},{7,8},{8,9},{9,10},{10,1... | collective-permute-start | bytes 589832 | tf_op jit(solution)/shard_map/ppermute | solution.py:246
  47.6 59.2 %copy-start.2 = (f32[128]{0:T(128)S(1)}, f32[128]{0:T(128)}, u32[]{:S(2)}) copy-start(f32[128]{0:T(128)} %param.15) | copy-start | bytes 1540
  47.6 1.6 %copy-start.1 = (f32[16,128,256]{2,1,0:T(8,128)S(1)}, f32[16,128,256]{2,1,0:T(8,128)}, u32[]{:S(2)}) copy-start(f32[16,128,256]{2,1,0:T(8,128)} %get-tuple-element.8.sum_ref) | copy-start | bytes 6291460
  106.9 3.4 %copy-start = (f32[16,512,256]{2,1,0:T(8,128)S(1)}, f32[16,512,256]{2,1,0:T(8,128)}, u32[]{:S(2)}) copy-start(f32[16,512,256]{2,1,0:T(8,128)} %get-tuple-element.7.part_ref) | copy-start | bytes 25165828
